TPU v7x, 32 devices: a whole 2x2x4 slice. The times are simulated.
32 devices in a mesh: dp: 4 (over z), expert: 8 (over y, x, core).
Axes of the slice: x: 2, y: 2, z: 4, core: 2. Of those that a mesh axis runs over, the one named last changes fastest.
Arguments:
- tokens: bfloat16 [8192, 1024], P(('dp', 'expert')), may hold values from -6 to 6
- routes: int32 [8192, 8], P(('dp', 'expert')), may hold values from 0 to 31, all different within a row; in each aligned block of 256 rows (0 to 255, 256 to 511, ...) at most 128 rows name the same one
- lengths: int32 [32, 4], P(('dp', 'expert')), may hold values from 1 to 192, 256 in all within a row
- query_weight: bfloat16 [1024, 1024], P('dp'), may hold values from -0.1875 to 0.1875
- key_weight: bfloat16 [1024, 512], P('dp'), may hold values from -0.1875 to 0.1875
- value_weight: bfloat16 [1024, 512], P('dp'), may hold values from -0.1875 to 0.1875
- output_weight: bfloat16 [1024, 1024], P('dp'), may hold values from -1 to 1
- router_weight: bfloat16 [1024, 32], P('dp'), may hold values from -0.09375 to 0.09375
- first_gain: bfloat16 [1024], P('dp'), may hold values from 0.5 to 1.5
- second_gain: bfloat16 [1024], P('dp'), may hold values from 0.5 to 1.5
- expert_gate: bfloat16 [32, 1024, 512], P('expert', 'dp'), may hold values from -0.1875 to 0.1875
- expert_up: bfloat16 [32, 1024, 512], P('expert', 'dp'), may hold values from -0.1875 to 0.1875
- expert_down: bfloat16 [32, 512, 1024], P('expert', None, 'dp'), may hold values from -1 to 1
- cotangent: bfloat16 [8192, 1024], P(('dp', 'expert')), may hold values from -6 to 6
Outputs:
- output: bfloat16 [8192, 1024], P(('dp', 'expert'))
- input_grad: float32 [8192, 1024], P(('dp', 'expert'))
- query_grad: float32 [1024, 1024], P('dp')
- key_grad: float32 [1024, 512], P('dp')
- value_grad: float32 [1024, 512], P('dp')
- output_grad: float32 [1024, 1024], P('dp')
- router_grad: float32 [1024, 32], P('dp')
- first_gain_grad: float32 [1024], P('dp')
- second_gain_grad: float32 [1024], P('dp')
- gate_grad: float32 [32, 1024, 512], P('expert', 'dp')
- up_grad: float32 [32, 1024, 512], P('expert', 'dp')
- down_grad: float32 [32, 512, 1024], P('expert', None, 'dp')
Inputs may be any that keep to these rules, and one draw needn't show every extreme that they name: `routes`: among the 256 rows of one device no expert is named more than 128 times, a bound that some block reaches; a row names 8 different experts. `lengths`: each row sums to 256; the largest length is 192.
All inputs are finite; a program needn't handle non-finite values.
Results may differ from a plain program's by a relative error of at most 0.02.
Values may be sent and summed in bfloat16 or wider, within the bound.
No kernel may reach another device: no remote copies, remote signals or barrier semaphores. Data moves between devices by JAX's collectives and lax.ppermute only.
A program may use at most 192 MiB of HBM per device.

v0:
```python
import jax
import jax.numpy as jnp
from jax import lax
from jax.sharding import PartitionSpec as P

D = 1024
HEADS = 16
KV_HEADS = 8
HEAD_DIM = 64
EXPERTS = 32
TOPK = 8
CAP = 128


EPSILON = 1e-06
THETA = 10000.0


def rotate_half(values):
    middle = values.shape[-1] // 2
    return jnp.concatenate([-values[..., middle:], values[..., :middle]], axis=-1)


def layout_tables(length_row, count):
    places = jnp.arange(count, dtype=jnp.int32)
    ends = jnp.cumsum(length_row)
    passed = places[:, None] >= ends[None, :]
    segment = jnp.sum(passed.astype(jnp.int32), axis=1)
    begins = jnp.sum(jnp.where(passed, length_row[None, :], 0), axis=1)
    position = (places - begins).astype(jnp.float32)
    frequency = THETA ** (-(jnp.arange(HEAD_DIM // 2, dtype=jnp.float32) * 2.0 / HEAD_DIM))
    angles = position[:, None] * frequency[None, :]
    cosine = jnp.concatenate([jnp.cos(angles), jnp.cos(angles)], axis=-1)
    sine = jnp.concatenate([jnp.sin(angles), jnp.sin(angles)], axis=-1)
    return (segment, cosine, sine)


def slot_layout(route_rows):
    flat_ids = route_rows.reshape(-1)
    count = flat_ids.shape[0]
    hits = (flat_ids[:, None] == jnp.arange(EXPERTS, dtype=jnp.int32)[None, :]).astype(jnp.int32)
    earlier = jnp.cumsum(hits, axis=0) - hits
    placed = jnp.sum(earlier * hits, axis=1)
    slot_of = flat_ids * CAP + placed
    source_row = jnp.arange(count, dtype=jnp.int32) // TOPK
    holder = jnp.zeros((EXPERTS * CAP,), jnp.int32).at[slot_of].set(source_row)
    filled = jnp.zeros((EXPERTS * CAP,), jnp.int32).at[slot_of].set(jnp.ones((count,), jnp.int32))
    return (slot_of, holder, filled)


def apply_rope(values, cosine, sine):
    return values * cosine[:, None, :] + rotate_half(values) * sine[:, None, :]


def rope_back(grads, cosine, sine):
    return grads * cosine[:, None, :] - rotate_half(grads * sine[:, None, :])


def contract_rows(left, right):
    return lax.dot_general(
        left, right, (((0,), (0,)), ((), ())), preferred_element_type=jnp.float32
    )


def times_transpose(left, right):
    return lax.dot_general(
        left, right, (((1,), (1,)), ((), ())), preferred_element_type=jnp.float32
    )


def on_device(
    tokens,
    routes,
    lengths,
    query_weight,
    key_weight,
    value_weight,
    output_weight,
    router_weight,
    first_gain,
    second_gain,
    expert_gate,
    expert_up,
    expert_down,
    cotangent,
):
    full_q, full_k, full_v, full_o, full_router, gain_one, gain_two = (
        lax.all_gather(query_weight, "dp", axis=0, tiled=True),
        lax.all_gather(key_weight, "dp", axis=0, tiled=True),
        lax.all_gather(value_weight, "dp", axis=0, tiled=True),
        lax.all_gather(output_weight, "dp", axis=0, tiled=True),
        lax.all_gather(router_weight, "dp", axis=0, tiled=True),
        lax.all_gather(first_gain, "dp", axis=0, tiled=True),
        lax.all_gather(second_gain, "dp", axis=0, tiled=True),
    )
    full_gate, full_up, full_down = (
        lax.all_gather(expert_gate, "dp", axis=1, tiled=True),
        lax.all_gather(expert_up, "dp", axis=1, tiled=True),
        lax.all_gather(expert_down, "dp", axis=2, tiled=True),
    )
    tok_count = tokens.shape[0]
    groups = HEADS // KV_HEADS
    scale = HEAD_DIM ** (-0.5)
    block_rows = min(512, tok_count)
    block_count = tok_count // block_rows
    owners = lax.axis_size("expert")
    local_count = full_gate.shape[0]
    segment, cosine, sine = layout_tables(lengths[0], tok_count)
    places = jnp.arange(tok_count, dtype=jnp.int32)
    inputs = tokens.astype(jnp.float32)
    gain_a = gain_one.astype(jnp.float32)
    gain_b = gain_two.astype(jnp.float32)
    scale_one = lax.rsqrt(jnp.mean(inputs * inputs, axis=-1, keepdims=True) + EPSILON)
    normed_one = (inputs * scale_one * gain_a).astype(jnp.bfloat16)
    q_lin = jnp.dot(normed_one, full_q, preferred_element_type=jnp.float32)
    k_lin = jnp.dot(normed_one, full_k, preferred_element_type=jnp.float32)
    v_lin = jnp.dot(normed_one, full_v, preferred_element_type=jnp.float32)
    queries = (apply_rope(q_lin.reshape(tok_count, HEADS, HEAD_DIM), cosine, sine) * scale).astype(
        jnp.bfloat16
    )
    keys = apply_rope(k_lin.reshape(tok_count, KV_HEADS, HEAD_DIM), cosine, sine).astype(
        jnp.bfloat16
    )
    values = v_lin.reshape(tok_count, KV_HEADS, HEAD_DIM).astype(jnp.bfloat16)
    query_blocks = queries.reshape(block_count, block_rows, KV_HEADS, groups, HEAD_DIM)
    seg_blocks = segment.reshape(block_count, block_rows)
    place_blocks = places.reshape(block_count, block_rows)

    def allowed_pairs(seg_query, place_query):
        return (seg_query[:, None] == segment[None, :]) & (places[None, :] <= place_query[:, None])

    def forward_block(pieces):
        q_block, seg_query, place_query = pieces
        scores = jnp.einsum("qhgd,khd->hgqk", q_block, keys, preferred_element_type=jnp.float32)
        scores = jnp.where(allowed_pairs(seg_query, place_query)[None, None], scores, -1e30)
        highest = jnp.max(scores, axis=-1, keepdims=True)
        raised = jnp.exp(scores - highest)
        totals = jnp.sum(raised, axis=-1, keepdims=True)
        probs = (raised / totals).astype(jnp.bfloat16)
        mixed = jnp.einsum("hgqk,khd->qhgd", probs, values, preferred_element_type=jnp.float32)
        return (mixed.reshape(block_rows, HEADS * HEAD_DIM), (highest + jnp.log(totals))[..., 0])

    mixed_all, log_totals = lax.map(forward_block, (query_blocks, seg_blocks, place_blocks))
    attended = mixed_all.reshape(tok_count, HEADS * HEAD_DIM).astype(jnp.bfloat16)
    residual = inputs + jnp.dot(attended, full_o, preferred_element_type=jnp.float32)
    scale_two = lax.rsqrt(jnp.mean(residual * residual, axis=-1, keepdims=True) + EPSILON)
    normed_two = (residual * scale_two * gain_b).astype(jnp.bfloat16)
    logits = jnp.dot(normed_two, full_router, preferred_element_type=jnp.float32)
    choose = (routes[:, :, None] == jnp.arange(EXPERTS, dtype=jnp.int32)[None, None, :]).astype(
        jnp.float32
    )
    chosen = jnp.sum(choose * logits[:, None, :], axis=-1)
    top_chosen = jnp.max(chosen, axis=-1, keepdims=True)
    raised_gates = jnp.exp(chosen - top_chosen)
    gates = raised_gates / jnp.sum(raised_gates, axis=-1, keepdims=True)
    slot_of, holder, filled = slot_layout(routes)
    occupied = filled[:, None] > 0
    outgoing = jnp.where(occupied, normed_two[holder], jnp.zeros((), jnp.bfloat16)).reshape(
        owners, local_count, CAP, D
    )
    arrived = lax.all_to_all(outgoing, "expert", split_axis=0, concat_axis=0, tiled=True)
    gate_pre = jnp.einsum("sjcd,jdf->sjcf", arrived, full_gate, preferred_element_type=jnp.float32)
    up_pre = jnp.einsum("sjcd,jdf->sjcf", arrived, full_up, preferred_element_type=jnp.float32)
    hidden = (gate_pre * jax.nn.sigmoid(gate_pre) * up_pre).astype(jnp.bfloat16)
    produced = jnp.einsum(
        "sjcf,jfd->sjcd", hidden, full_down, preferred_element_type=jnp.float32
    ).astype(jnp.bfloat16)
    returned = lax.all_to_all(produced, "expert", split_axis=0, concat_axis=0, tiled=True)
    picked = returned.reshape(EXPERTS * CAP, D)[slot_of].reshape(tok_count, TOPK, D)
    mixture = jnp.sum(gates[:, :, None] * picked, axis=1)
    output = (residual + mixture).astype(jnp.bfloat16)
    upstream = cotangent.astype(jnp.float32)
    gate_back = jnp.sum(upstream[:, None, :] * picked, axis=-1)
    chosen_back = gates * (gate_back - jnp.sum(gates * gate_back, axis=-1, keepdims=True))
    logit_back = jnp.sum(chosen_back[:, :, None] * choose, axis=1).astype(jnp.bfloat16)
    router_part = contract_rows(normed_two, logit_back)
    normed_back = times_transpose(logit_back, full_router)
    slot_gate = jnp.zeros((EXPERTS * CAP,), jnp.float32).at[slot_of].set(gates.reshape(-1))
    slot_back = (
        jnp.where(occupied, slot_gate[:, None] * upstream[holder], 0.0)
        .astype(jnp.bfloat16)
        .reshape(owners, local_count, CAP, D)
    )
    rows_in, grads_in = (
        lax.all_to_all(outgoing, "expert", split_axis=0, concat_axis=0, tiled=True),
        lax.all_to_all(slot_back, "expert", split_axis=0, concat_axis=0, tiled=True),
    )
    gate_again = jnp.einsum(
        "sjcd,jdf->sjcf", rows_in, full_gate, preferred_element_type=jnp.float32
    )
    up_again = jnp.einsum("sjcd,jdf->sjcf", rows_in, full_up, preferred_element_type=jnp.float32)
    sigma = jax.nn.sigmoid(gate_again)
    activated = gate_again * sigma
    hidden_again = (activated * up_again).astype(jnp.bfloat16)
    hidden_back = jnp.einsum(
        "sjcd,jfd->sjcf", grads_in, full_down, preferred_element_type=jnp.float32
    )
    gate_slope = (hidden_back * up_again * sigma * (1.0 + gate_again * (1.0 - sigma))).astype(
        jnp.bfloat16
    )
    up_slope = (hidden_back * activated).astype(jnp.bfloat16)
    down_part = jnp.einsum(
        "sjcf,sjcd->jfd", hidden_again, grads_in, preferred_element_type=jnp.float32
    )
    gate_part = jnp.einsum(
        "sjcd,sjcf->jdf", rows_in, gate_slope, preferred_element_type=jnp.float32
    )
    up_part = jnp.einsum("sjcd,sjcf->jdf", rows_in, up_slope, preferred_element_type=jnp.float32)
    entry_back = jnp.einsum(
        "sjcf,jdf->sjcd", gate_slope, full_gate, preferred_element_type=jnp.float32
    )
    entry_back = (
        entry_back
        + jnp.einsum("sjcf,jdf->sjcd", up_slope, full_up, preferred_element_type=jnp.float32)
    ).astype(jnp.bfloat16)
    sent_back = lax.all_to_all(entry_back, "expert", split_axis=0, concat_axis=0, tiled=True)
    gathered_back = sent_back.reshape(EXPERTS * CAP, D)[slot_of].reshape(tok_count, TOPK, D)
    normed_back = normed_back + jnp.sum(gathered_back.astype(jnp.float32), axis=1)
    gate_grad, up_grad, down_grad = (
        lax.psum_scatter(
            gate_part.astype(jnp.bfloat16), "dp", scatter_dimension=1, tiled=True
        ).astype(jnp.float32),
        lax.psum_scatter(
            up_part.astype(jnp.bfloat16), "dp", scatter_dimension=1, tiled=True
        ).astype(jnp.float32),
        lax.psum_scatter(
            down_part.astype(jnp.bfloat16), "dp", scatter_dimension=2, tiled=True
        ).astype(jnp.float32),
    )
    scaled_two = normed_back * gain_b
    second_gain_part = jnp.sum(normed_back * residual * scale_two, axis=0)
    residual_back = (
        upstream
        + scale_two * scaled_two
        - residual * scale_two**3 * jnp.mean(scaled_two * residual, axis=-1, keepdims=True)
    )
    branch_back = residual_back.astype(jnp.bfloat16)
    output_part = contract_rows(attended, branch_back)
    attended_back = times_transpose(branch_back, full_o).astype(jnp.bfloat16)
    back_blocks = attended_back.reshape(block_count, block_rows, KV_HEADS, groups, HEAD_DIM)

    def backward_block(carry, pieces):
        key_total, value_total = carry
        q_block, g_block, lse_block, seg_query, place_query = pieces
        scores = jnp.einsum("qhgd,khd->hgqk", q_block, keys, preferred_element_type=jnp.float32)
        allowed = allowed_pairs(seg_query, place_query)[None, None]
        probs = jnp.where(
            allowed, jnp.exp(jnp.where(allowed, scores, -1e30) - lse_block[..., None]), 0.0
        )
        prob_back = jnp.einsum(
            "qhgd,khd->hgqk", g_block, values, preferred_element_type=jnp.float32
        )
        spread = jnp.sum(prob_back * probs, axis=-1, keepdims=True)
        score_back = (probs * (prob_back - spread)).astype(jnp.bfloat16)
        query_back = jnp.einsum(
            "hgqk,khd->qhgd", score_back, keys, preferred_element_type=jnp.float32
        )
        key_total = key_total + jnp.einsum(
            "hgqk,qhgd->khd", score_back, q_block, preferred_element_type=jnp.float32
        )
        value_total = value_total + jnp.einsum(
            "hgqk,qhgd->khd",
            probs.astype(jnp.bfloat16),
            g_block,
            preferred_element_type=jnp.float32,
        )
        return ((key_total, value_total), query_back.reshape(block_rows, HEADS, HEAD_DIM))

    empty_kv = jnp.zeros((tok_count, KV_HEADS, HEAD_DIM), jnp.float32)
    (key_sum, value_sum), query_backs = lax.scan(
        backward_block,
        (empty_kv, empty_kv),
        (query_blocks, back_blocks, log_totals, seg_blocks, place_blocks),
    )
    q_back = (
        (rope_back(query_backs.reshape(tok_count, HEADS, HEAD_DIM), cosine, sine) * scale)
        .astype(jnp.bfloat16)
        .reshape(tok_count, HEADS * HEAD_DIM)
    )
    k_back = (
        rope_back(key_sum, cosine, sine)
        .astype(jnp.bfloat16)
        .reshape(tok_count, KV_HEADS * HEAD_DIM)
    )
    v_back = value_sum.astype(jnp.bfloat16).reshape(tok_count, KV_HEADS * HEAD_DIM)
    query_part = contract_rows(normed_one, q_back)
    key_part = contract_rows(normed_one, k_back)
    value_part = contract_rows(normed_one, v_back)
    first_back = (
        times_transpose(q_back, full_q)
        + times_transpose(k_back, full_k)
        + times_transpose(v_back, full_v)
    )
    scaled_one = first_back * gain_a
    first_gain_part = jnp.sum(first_back * inputs * scale_one, axis=0)
    input_grad = (
        residual_back
        + scale_one * scaled_one
        - inputs * scale_one**3 * jnp.mean(scaled_one * inputs, axis=-1, keepdims=True)
    )
    summed = (
        lax.psum(query_part.astype(jnp.bfloat16), "expert").astype(jnp.float32),
        lax.psum(key_part.astype(jnp.bfloat16), "expert").astype(jnp.float32),
        lax.psum(value_part.astype(jnp.bfloat16), "expert").astype(jnp.float32),
        lax.psum(output_part.astype(jnp.bfloat16), "expert").astype(jnp.float32),
        lax.psum(router_part.astype(jnp.bfloat16), "expert").astype(jnp.float32),
        lax.psum(first_gain_part.astype(jnp.bfloat16), "expert").astype(jnp.float32),
        lax.psum(second_gain_part.astype(jnp.bfloat16), "expert").astype(jnp.float32),
    )
    finals = (
        lax.psum_scatter(
            summed[0].astype(jnp.bfloat16), "dp", scatter_dimension=0, tiled=True
        ).astype(jnp.float32),
        lax.psum_scatter(
            summed[1].astype(jnp.bfloat16), "dp", scatter_dimension=0, tiled=True
        ).astype(jnp.float32),
        lax.psum_scatter(
            summed[2].astype(jnp.bfloat16), "dp", scatter_dimension=0, tiled=True
        ).astype(jnp.float32),
        lax.psum_scatter(
            summed[3].astype(jnp.bfloat16), "dp", scatter_dimension=0, tiled=True
        ).astype(jnp.float32),
        lax.psum_scatter(
            summed[4].astype(jnp.bfloat16), "dp", scatter_dimension=0, tiled=True
        ).astype(jnp.float32),
        lax.psum_scatter(
            summed[5].astype(jnp.bfloat16), "dp", scatter_dimension=0, tiled=True
        ).astype(jnp.float32),
        lax.psum_scatter(
            summed[6].astype(jnp.bfloat16), "dp", scatter_dimension=0, tiled=True
        ).astype(jnp.float32),
    )
    return (
        output,
        input_grad,
        finals[0],
        finals[1],
        finals[2],
        finals[3],
        finals[4],
        finals[5],
        finals[6],
        gate_grad,
        up_grad,
        down_grad,
    )


def solution(mesh):
    return jax.shard_map(
        on_device,
        mesh=mesh,
        in_specs=(
            P(("dp", "expert"), None),
            P(("dp", "expert"), None),
            P(("dp", "expert"), None),
            P("dp", None),
            P("dp", None),
            P("dp", None),
            P("dp", None),
            P("dp", None),
            P("dp"),
            P("dp"),
            P("expert", "dp", None),
            P("expert", "dp", None),
            P("expert", None, "dp"),
            P(("dp", "expert"), None),
        ),
        out_specs=(
            P(("dp", "expert"), None),
            P(("dp", "expert"), None),
            P("dp", None),
            P("dp", None),
            P("dp", None),
            P("dp", None),
            P("dp", None),
            P("dp"),
            P("dp"),
            P("expert", "dp", None),
            P("expert", "dp", None),
            P("expert", None, "dp"),
        ),
        check_vma=False,
    )
```

profile of v0, /device:TPU:0, one launch (start us, length us, event | category | flops | bytes accessed | tf_op | source)
XLA Modules:
  0.0 1149.8 jit_solution(3786969879521355158)
XLA Ops:
  14.8 12.7 %all-gather = bf16[4,1,256]{2,1,0:T(2,128)(2,1)S(1)} all-gather(bf16[1,1,256]{2,1,0:T(2,128)(2,1)S(1)} %reshape.461), channel_id=1, replica_groups=mesh['dp'=4,'expert'=8] {'dp'}, dimensions={0}, use_global_device_ids=true | all-gather | bytes 2560 | tf_op jit(solution)/shard_map/all_gather | solution.py:93
  29.9 7.7 all-gather.1
  37.6 9.1 reduce-window.19
  47.8 8.1 scatter_custom_fusion.1
  55.9 8.1 scatter_custom_fusion
  66.1 3.2 all-gather.10.cloned.1.call-done
  71.3 45.1 %all-gather.14.cloned.1.call-done = bf16[1024,1024]{1,0:T(8,128)(2,1)} async-done(((bf16[256,1024]{1,0:T(8,128)(2,1)}), bf16[1024,1024]{1,0:T(8,128)(2,1)}) %all-gather.14.cloned.1.call-update) | async-done | bytes 2097168 | tf_op jit(solution)/shard_map/all_gather | solution.py:88
  124.0 38.5 %all-gather.16.cloned.1.call-done = bf16[1024,1024]{1,0:T(8,128)(2,1)} async-done(((bf16[256,1024]{1,0:T(8,128)(2,1)}), bf16[1024,1024]{1,0:T(8,128)(2,1)}) %all-gather.16.cloned.1.call-update) | async-done | bytes 2097168 | tf_op jit(solution)/shard_map/all_gather | solution.py:91
  166.1 18.3 %gather_fusion = bf16[4096,1024]{1,0:T(8,128)(2,1)} fusion(bf16[256,1024]{1,0:T(8,128)(2,1)S(1)} %multiply_convert_fusion, s32[4096]{0:T(1024)S(1)} %fusion.79), kind=kCustom, calls=%fused_computation | custom fusion | bytes 16793600 | tf_op jit(solution)/shard_map/gather | solution.py:158
  184.4 7.2 broadcast_select_fusion
  191.6 5.1 all-to-all-start
  197.4 18.6 %gather_fusion.2 = f32[4096,1024]{1,0:T(8,128)} fusion(f32[256,1024]{1,0:T(8,128)S(1)} %convert_element_type.235, s32[4096]{0:T(1024)S(1)} %fusion.79), kind=kCustom, calls=%fused_computation.2 | custom fusion | bytes 33570816 | tf_op jit(solution)/shard_map/gather | solution.py:180
  216.0 13.8 %all_gather.36 = bf16[1024,32]{0,1:T(8,128)(2,1)S(1)} all-gather(bf16[256,32]{0,1:T(8,128)(2,1)S(1)} %copy-done.44), channel_id=1, replica_groups=mesh['dp'=4,'expert'=8] {'dp'}, dimensions={0}, use_global_device_ids=true | all-gather | bytes 81920 | tf_op jit(solution)/shard_map/all_gather | solution.py:92
  230.4 8.1 scatter_custom_fusion.2
  238.5 9.3 select_convert_fusion
  247.8 42.9 %all-to-all-done = bf16[8,4,128,1024]{3,2,1,0:T(8,128)(2,1)} async-done(((bf16[8,4,128,1024]{3,2,1,0:T(8,128)(2,1)}), bf16[8,4,128,1024]{3,2,1,0:T(8,128)(2,1)}, u32[]{:S(2)}, u32[]{:S(2)}) %all-to-all-start) | async-done | bytes 8388640 | tf_op jit(solution)/shard_map/all_to_all | solution.py:161
  290.8 5.0 all-to-all-start.2
  296.6 12.4 %fusion.16 = f32[4,8,128,512]{3,2,1,0:T(8,128)} fusion(bf16[8,4,128,1024]{3,2,1,0:T(8,128)(2,1)} %all-to-all-done, bf16[4,1024,512]{2,1,0:T(8,128)(2,1)} %all-gather.20.cloned.1.call-done), kind=kOutput, calls=%fused_computation.39 | convolution fusion | flops 4294967296 | bytes 20971520 | tf_op jit(solution)/shard_map/sjcd,jdf->sjcf/dot_general | solution.py:163
  309.0 16.2 %all-gather.18.cloned.1.call-done = bf16[4,1024,512]{2,1,0:T(8,128)(2,1)} async-done(((bf16[4,256,512]{2,1,0:T(8,128)(2,1)}), bf16[4,1024,512]{2,1,0:T(8,128)(2,1)}) %all-gather.18.cloned.1.call-update) | async-done | bytes 4194320 | tf_op jit(solution)/shard_map/all_gather | solution.py:97
  325.2 12.3 %fusion.18 = f32[4,8,128,512]{3,2,1,0:T(8,128)} fusion(bf16[8,4,128,1024]{3,2,1,0:T(8,128)(2,1)} %all-to-all-done, bf16[4,1024,512]{2,1,0:T(8,128)(2,1)} %all-gather.18.cloned.1.call-done), kind=kOutput, calls=%fused_computation.41 | convolution fusion | flops 4294967296 | bytes 20971520 | tf_op jit(solution)/shard_map/sjcd,jdf->sjcf/dot_general | solution.py:162
  337.5 68.4 %all-gather.22.cloned.1.call-done = bf16[4,512,1024]{2,1,0:T(8,128)(2,1)} async-done(((bf16[4,512,256]{2,1,0:T(8,128)(2,1)}), bf16[4,512,1024]{2,1,0:T(8,128)(2,1)}) %all-gather.22.cloned.1.call-update) | async-done | bytes 4194320 | tf_op jit(solution)/shard_map/all_gather | solution.py:99
  405.9 16.7 %fusion.6 = (bf16[8,4,128,512]{3,2,0,1:T(8,128)(2,1)}, bf16[8,4,128,512]{3,2,0,1:T(8,128)(2,1)}, bf16[8,4,128,512]{3,2,0,1:T(8,128)(2,1)}) fusion(f32[4,8,128,512]{3,2,1,0:T(8,128)} %fusion.18, f32[4,8,128,512]{3,2,1,0:T(8,128)} %fusion.16, bf16[4,512,1024]{2,1,0:T(8,128)(2,1)} %all-gather.22.cloned.1.call-done, bf16[8,4,128,1024]{3,2,1,0:T(8,128)(2,1)} %all-to-all-done.2), kind=kOutput, calls=%fused_computation.23 | convolution fusion | flops 4326424576 | bytes 41943040 | tf_op jit(solution)/shard_map/sjcd,jfd->sjcf/dot_general | solution.py:195
  422.6 11.2 convert_bitcast_fusion
  433.8 8.2 copy.135
  442.0 5.4 all-to-all-start.1
  447.5 13.8 %fusion.25 = f32[4,8,128,1024]{3,2,1,0:T(8,128)} fusion(bf16[8,4,128,512]{3,2,0,1:T(8,128)(2,1)} %get-tuple-element.99, bf16[4,1024,512]{2,1,0:T(8,128)(2,1)} %all-gather.18.cloned.1.call-done), kind=kOutput, calls=%fused_computation.50 | convolution fusion | flops 4294967296 | bytes 25165824 | tf_op jit(solution)/shard_map/sjcf,jdf->sjcd/dot_general | solution.py:209
  461.2 12.6 %fusion.2 = bf16[8,4,128,1024]{3,2,0,1:T(8,128)(2,1)} fusion(f32[4,8,128,1024]{3,2,1,0:T(8,128)} %fusion.25, bf16[8,4,128,512]{3,2,0,1:T(8,128)(2,1)} %get-tuple-element.98, bf16[4,1024,512]{2,1,0:T(8,128)(2,1)} %all-gather.20.cloned.1.call-done), kind=kOutput, calls=%fused_computation.13 | convolution fusion | flops 4303355904 | bytes 33554432 | tf_op jit(solution)/shard_map/sjcf,jdf->sjcd/dot_general | solution.py:214
  473.8 8.2 copy.140
  482.0 59.5 %all-to-all-done.1 = bf16[8,4,128,1024]{3,2,1,0:T(8,128)(2,1)} async-done(((bf16[8,4,128,1024]{3,2,1,0:T(8,128)(2,1)}), bf16[8,4,128,1024]{3,2,1,0:T(8,128)(2,1)}, u32[]{:S(2)}, u32[]{:S(2)}) %all-to-all-start.1) | async-done | bytes 8388640 | tf_op jit(solution)/shard_map/all_to_all | solution.py:168
  541.5 5.0 all-to-all-start.3
  546.7 15.6 %gather_fusion.1 = bf16[2048,1024]{1,0:T(8,128)(2,1)} fusion(bf16[4096,1024]{1,0:T(8,128)(2,1)} %bitcast.34, s32[2048]{0:T(1024)S(1)} %broadcast_clamp_fusion), kind=kCustom, calls=%fused_computation.1 | custom fusion | bytes 8396800 | tf_op jit(solution)/shard_map/gather | solution.py:169
  562.3 5.1 fusion.1
  567.6 73.0 %all-to-all-done.3 = bf16[8,4,128,1024]{3,2,1,0:T(8,128)(2,1)} async-done(((bf16[8,4,128,1024]{3,2,1,0:T(8,128)(2,1)}), bf16[8,4,128,1024]{3,2,1,0:T(8,128)(2,1)}, u32[]{:S(2)}, u32[]{:S(2)}) %all-to-all-start.3) | async-done | bytes 8388640 | tf_op jit(solution)/shard_map/all_to_all | solution.py:216
  640.6 15.4 %gather_fusion.3 = bf16[2048,1024]{1,0:T(8,128)(2,1)} fusion(bf16[4096,1024]{1,0:T(8,128)(2,1)} %bitcast.44, s32[2048]{0:T(1024)S(1)} %broadcast_clamp_fusion), kind=kCustom, calls=%fused_computation.3 | custom fusion | bytes 8396800 | tf_op jit(solution)/shard_map/gather | solution.py:217
  656.1 5.6 convert_reduce_fusion
  670.6 3.8 fusion.20
  685.3 11.2 bitcast_convert_fusion
  696.8 11.1 bitcast_convert_fusion.2
  708.0 11.1 bitcast_convert_fusion.1
  726.1 42.0 %reduce-scatter.15.cloned.1.call-done = bf16[256,1024]{1,0:T(8,128)(2,1)} async-done(((bf16[1024,1024]{1,0:T(8,128)(2,1)}), bf16[256,1024]{1,0:T(8,128)(2,1)}) %reduce-scatter.15.cloned.1.call-update) | async-done | bytes 524304 | tf_op jit(solution)/shard_map/reduce_scatter | solution.py:311
  768.1 46.2 %reduce-scatter.21.cloned.1.call-done = bf16[256,1024]{1,0:T(8,128)(2,1)} async-done(((bf16[1024,1024]{1,0:T(8,128)(2,1)}), bf16[256,1024]{1,0:T(8,128)(2,1)}) %reduce-scatter.21.cloned.1.call-update) | async-done | bytes 524304 | tf_op jit(solution)/shard_map/reduce_scatter | solution.py:320
  816.6 9.9 all-reduce.4
  827.9 7.5 reduce-scatter.23.cloned.1.call-done
  835.4 23.0 %all-reduce.2 = (bf16[256,32]{0,1:T(8,128)(2,1)S(1)}, bf16[256]{0:T(256)(128)(2,1)S(1)}, bf16[256]{0:T(256)(128)(2,1)S(1)}) all-reduce(bf16[256,32]{0,1:T(8,128)(2,1)} %reduce-scatter.23.cloned.1.call-done, bf16[256]{0:T(256)(128)(2,1)S(1)} %dynamic-slice.2, ...), channel_id=1, replica_groups=mesh['dp'=4,'expert'=8] {'expert'}, use_global_device_ids=true, to_apply=%region_32.33 | all-reduce | flops 8704 | bytes 34816 | tf_op jit(solution)/shard_map/psum | solution.py:306
  860.2 52.6 %reduce-scatter.13.cloned.1.call-done = bf16[4,512,256]{2,1,0:T(8,128)(2,1)} async-done(((bf16[4,512,1024]{2,1,0:T(8,128)(2,1)}), bf16[4,512,256]{2,1,0:T(8,128)(2,1)}) %reduce-scatter.13.cloned.1.call-update) | async-done | bytes 1048592 | tf_op jit(solution)/shard_map/reduce_scatter | solution.py:226
  915.5 76.7 %reduce-scatter.9.cloned.1.call-done = bf16[4,256,512]{2,1,0:T(8,128)(2,1)} async-done(((bf16[4,1024,512]{2,1,0:T(8,128)(2,1)}), bf16[4,256,512]{2,1,0:T(8,128)(2,1)}) %reduce-scatter.9.cloned.1.call-update) | async-done | bytes 1048592 | tf_op jit(solution)/shard_map/reduce_scatter | solution.py:220
  995.0 76.7 %reduce-scatter.11.cloned.1.call-done = bf16[4,256,512]{2,1,0:T(8,128)(2,1)} async-done(((bf16[4,1024,512]{2,1,0:T(8,128)(2,1)}), bf16[4,256,512]{2,1,0:T(8,128)(2,1)}) %reduce-scatter.11.cloned.1.call-update) | async-done | bytes 1048592 | tf_op jit(solution)/shard_map/reduce_scatter | solution.py:223
  1074.6 60.4 %all-reduce.7.cloned.1.call-done = (bf16[256,1024]{1,0:T(8,128)(2,1)}, bf16[256,512]{1,0:T(8,128)(2,1)}, bf16[256,512]{1,0:T(8,128)(2,1)}, bf16[256,1024]{1,0:T(8,128)(2,1)}) async-done(((bf16[256,1024]{1,0:T(8,128)(2,1)}, bf16[256,512]{1,0:T(8,128)(2,1)}, bf16[256,512]{1,0:T(8,128)(2,1)}, bf16[256,1024]{1,0:T(8,128)(2,1)}), (bf16[256,1024]{1,0:T(8,128)(2,1)}, bf16[256,512]{1,0:T(8,128)(2,1)}, ...) | async-done | bytes 1572880 | tf_op jit(solution)/shard_map/psum | solution.py:302
  (229 shorter events, 76.1 us)
Async XLA Ops:
  7.2 57.1 %copy-start.2 = (bf16[256,1024]{1,0:T(8,128)(2,1)S(1)}, bf16[256,1024]{1,0:T(8,128)(2,1)}, u32[]{:S(2)}) copy-start(bf16[256,1024]{1,0:T(8,128)(2,1)} %param.14) | copy-start | bytes 1572868
  7.2 57.1 %all-gather.12.cloned.1.call-start = ((), (), s32[]{:S(2)}) async-start(), calls=%async_computation.13 | async-start | bytes 1310720 | tf_op jit(solution)/shard_map/all_gather | solution.py:89
  7.9 61.4 %all-gather.10.cloned.1.call-start = ((), (), s32[]{:S(2)}) async-start(), calls=%async_computation.12 | async-start | bytes 1310720 | tf_op jit(solution)/shard_map/all_gather | solution.py:90
  8.7 107.7 %all-gather.14.cloned.1.call-start = ((), (), s32[]{:S(2)}) async-start(), calls=%async_computation.14 | async-start | bytes 2621440 | tf_op jit(solution)/shard_map/all_gather | solution.py:88
  9.4 153.1 %all-gather.16.cloned.1.call-start = ((), (), s32[]{:S(2)}) async-start(), calls=%async_computation.15 | async-start | bytes 2621440 | tf_op jit(solution)/shard_map/all_gather | solution.py:91
  10.0 286.6 %all-gather.20.cloned.1.call-start = ((), (), s32[]{:S(2)}) async-start(), calls=%async_computation.17 | async-start | bytes 5242880 | tf_op jit(solution)/shard_map/all_gather | solution.py:98
  14.1 102.3 %copy-start.40 = (f32[256]{0:T(256)}, f32[256]{0:T(256)S(1)}, u32[]{:S(2)}) copy-start(f32[256]{0:T(256)S(1)} %get-tuple-element.114) | copy-start | bytes 3076
  27.5 88.9 %copy-start.29 = (f32[4,1,256]{2,1,0:T(1,128)}, f32[4,1,256]{2,1,0:T(1,128)S(1)}, u32[]{:S(2)}) copy-start(f32[4,1,256]{2,1,0:T(1,128)S(1)} %convert_element_type.274) | copy-start | bytes 12292
  29.2 92.5 %copy-start.19 = (pred[256,256]{0,1:T(8,128)(4,1)}, pred[256,256]{0,1:T(8,128)(4,1)S(1)}, u32[]{:S(2)}) copy-start(pred[256,256]{0,1:T(8,128)(4,1)S(1)} %fusion.77) | copy-start | bytes 196612
  37.6 128.0 %copy-start.36 = (f32[4,1,256]{2,1,0:T(1,128)}, f32[4,1,256]{2,1,0:T(1,128)S(1)}, u32[]{:S(2)}) copy-start(f32[4,1,256]{2,1,0:T(1,128)S(1)} %convert_element_type.275) | copy-start | bytes 12292
  64.2 54.9 %copy-start.21 = (f32[256,64]{0,1:T(8,128)}, f32[256,64]{0,1:T(8,128)S(1)}, u32[]{:S(2)}) copy-start(f32[256,64]{0,1:T(8,128)S(1)} %get-tuple-element.128) | copy-start | bytes 196612
  64.2 54.9 %copy-start.23 = (f32[256,64]{0,1:T(8,128)}, f32[256,64]{0,1:T(8,128)S(1)}, u32[]{:S(2)}) copy-start(f32[256,64]{0,1:T(8,128)S(1)} %get-tuple-element.127) | copy-start | bytes 196612
  71.2 48.2 %copy-start.11 = (bf16[256,8,64,1]{0,2,3,1:T(8,128)(2,1)}, bf16[256,8,64,1]{0,2,3,1:T(8,128)(2,1)S(1)}, u32[]{:S(2)}) copy-start(bf16[256,8,64,1]{0,2,3,1:T(8,128)(2,1)S(1)} %fusion.71) | copy-start | bytes 786436
  71.3 50.4 %copy-start.25 = (bf16[256,512]{0,1:T(8,128)(2,1)}, bf16[256,512]{0,1:T(8,128)(2,1)S(1)}, u32[]{:S(2)}) copy-start(bf16[256,512]{0,1:T(8,128)(2,1)S(1)} %copy.122) | copy-start | bytes 786436
  124.0 60.4 %copy-start.17 = (bf16[8,64,2,256]{3,1,2,0:T(8,128)(2,1)}, bf16[8,64,2,256]{3,1,2,0:T(8,128)(2,1)S(1)}, u32[]{:S(2)}) copy-start(bf16[8,64,2,256]{3,1,2,0:T(8,128)(2,1)S(1)} %fusion.47) | copy-start | bytes 1572868
  165.6 18.8 %copy-start.42 = (f32[256]{0:T(256)}, f32[256]{0:T(256)S(1)}, u32[]{:S(2)}) copy-start(f32[256]{0:T(256)S(1)} %get-tuple-element.116) | copy-start | bytes 3076
  191.6 5.7 copy-start.15
  191.6 99.2 %all-to-all-start = ((bf16[8,4,128,1024]{3,2,1,0:T(8,128)(2,1)}), bf16[8,4,128,1024]{3,2,1,0:T(8,128)(2,1)}, u32[]{:S(2)}, u32[]{:S(2)}) async-start(bf16[8,4,128,1024]{3,2,1,0:T(8,128)(2,1)} %broadcast_select_fusion), calls=%async_computation | async-start | bytes 16777216 | tf_op jit(solution)/shard_map/all_to_all | solution.py:161
  196.7 128.5 %all-gather.18.cloned.1.call-start = ((), (), s32[]{:S(2)}) async-start(), calls=%async_computation.16 | async-start | bytes 5242880 | tf_op jit(solution)/shard_map/all_gather | solution.py:97
  197.4 18.6 %copy-start.44 = (bf16[256,32]{0,1:T(8,128)(2,1)S(1)}, bf16[256,32]{0,1:T(8,128)(2,1)}, u32[]{:S(2)}) copy-start(bf16[256,32]{0,1:T(8,128)(2,1)} %param.21) | copy-start | bytes 49156
  197.4 32.7 %copy-start.35 = (s32[256,8]{0,1:T(8,128)S(1)}, s32[256,8]{0,1:T(8,128)}, u32[]{:S(2)}) copy-start(s32[256,8]{0,1:T(8,128)} %param.15) | copy-start | bytes 24580
  290.8 115.1 %all-to-all-start.2 = ((bf16[8,4,128,1024]{3,2,1,0:T(8,128)(2,1)}), bf16[8,4,128,1024]{3,2,1,0:T(8,128)(2,1)}, u32[]{:S(2)}, u32[]{:S(2)}) async-start(bf16[8,4,128,1024]{3,2,1,0:T(8,128)(2,1)} %select_convert_fusion), calls=%async_computation.2 | async-start | bytes 16777216 | tf_op jit(solution)/shard_map/all_to_all | solution.py:186
  295.8 110.1 %all-gather.22.cloned.1.call-start = ((), (), s32[]{:S(2)}) async-start(), calls=%async_computation.18 | async-start | bytes 5242880 | tf_op jit(solution)/shard_map/all_gather | solution.py:99
  442.0 99.5 %all-to-all-start.1 = ((bf16[8,4,128,1024]{3,2,1,0:T(8,128)(2,1)}), bf16[8,4,128,1024]{3,2,1,0:T(8,128)(2,1)}, u32[]{:S(2)}, u32[]{:S(2)}) async-start(bf16[8,4,128,1024]{3,2,1,0:T(8,128)(2,1)} %copy.135), calls=%async_computation.1 | async-start | bytes 16777216 | tf_op jit(solution)/shard_map/all_to_all | solution.py:168
  482.0 64.6 %copy-start.32 = (f32[8,2,256]{2,1,0:T(2,128)S(1)}, f32[8,2,256]{2,1,0:T(2,128)}, u32[]{:S(2)}) copy-start(f32[8,2,256]{2,1,0:T(2,128)} %copy-done.31) | copy-start | bytes 49156
  482.0 64.6 %copy-start.39 = (f32[8,2,256]{2,1,0:T(2,128)S(1)}, f32[8,2,256]{2,1,0:T(2,128)}, u32[]{:S(2)}) copy-start(f32[8,2,256]{2,1,0:T(2,128)} %copy-done.38) | copy-start | bytes 49156
  541.5 99.1 %all-to-all-start.3 = ((bf16[8,4,128,1024]{3,2,1,0:T(8,128)(2,1)}), bf16[8,4,128,1024]{3,2,1,0:T(8,128)(2,1)}, u32[]{:S(2)}, u32[]{:S(2)}) async-start(bf16[8,4,128,1024]{3,2,1,0:T(8,128)(2,1)} %copy.140), calls=%async_computation.3 | async-start | bytes 16777216 | tf_op jit(solution)/shard_map/all_to_all | solution.py:216
  546.6 179.6 %reduce-scatter.19.cloned.1.call-start = ((), (), s32[]{:S(2)}) async-start(), calls=%async_computation.24 | async-start | bytes 1310720 | tf_op jit(solution)/shard_map/reduce_scatter | solution.py:317
  567.6 94.1 %copy-start.33 = (bf16[256,32]{0,1:T(8,128)(2,1)}, bf16[256,32]{0,1:T(8,128)(2,1)S(1)}, u32[]{:S(2)}) copy-start(bf16[256,32]{0,1:T(8,128)(2,1)S(1)} %select_reduce_fusion) | copy-start | bytes 49156
  656.0 5.6 copy-start.7
  656.0 5.6 copy-start.37
  656.1 5.6 copy-start.43
  656.1 6.2 copy-start.16
  656.1 6.2 copy-start.46
  665.5 5.1 copy-start.26
  668.7 5.7 copy-start.27
  670.3 55.8 %reduce-scatter.17.cloned.1.call-start = ((), (), s32[]{:S(2)}) async-start(), calls=%async_computation.23 | async-start | bytes 1310720 | tf_op jit(solution)/shard_map/reduce_scatter | solution.py:314
  670.6 3.8 copy-start.1
  679.0 89.1 %reduce-scatter.15.cloned.1.call-start = ((), (), s32[]{:S(2)}) async-start(), calls=%async_computation.22 | async-start | bytes 2621440 | tf_op jit(solution)/shard_map/reduce_scatter | solution.py:311
  682.2 132.1 %reduce-scatter.21.cloned.1.call-start = ((), (), s32[]{:S(2)}) async-start(), calls=%async_computation.25 | async-start | bytes 2621440 | tf_op jit(solution)/shard_map/reduce_scatter | solution.py:320
  684.3 151.1 %reduce-scatter.23.cloned.1.call-start = ((), (), s32[]{:S(2)}) async-start(), calls=%async_computation.26 | async-start | bytes 81920 | tf_op jit(solution)/shard_map/reduce_scatter | solution.py:323
  685.2 227.5 %reduce-scatter.13.cloned.1.call-start = ((), (), s32[]{:S(2)}) async-start(), calls=%async_computation.21 | async-start | bytes 5242880 | tf_op jit(solution)/shard_map/reduce_scatter | solution.py:226
  696.5 295.7 %reduce-scatter.9.cloned.1.call-start = ((), (), s32[]{:S(2)}) async-start(), calls=%async_computation.19 | async-start | bytes 5242880 | tf_op jit(solution)/shard_map/reduce_scatter | solution.py:220
  707.9 363.8 %reduce-scatter.11.cloned.1.call-start = ((), (), s32[]{:S(2)}) async-start(), calls=%async_computation.20 | async-start | bytes 5242880 | tf_op jit(solution)/shard_map/reduce_scatter | solution.py:223
  719.1 4.3 copy-start.14
  719.1 415.8 %all-reduce.7.cloned.1.call-start = ((), (), s32[]{:S(2)}) async-start(), calls=%async_computation.27 | async-start | bytes 3145728 | tf_op jit(solution)/shard_map/psum | solution.py:302
  721.0 93.4 %copy-start.28 = (bf16[8,64,256]{2,1,0:T(8,128)(2,1)S(1)}, bf16[8,64,256]{2,1,0:T(8,128)(2,1)}, u32[]{:S(2)}) copy-start(bf16[8,64,256]{2,1,0:T(8,128)(2,1)} %copy-done.27) | copy-start | bytes 786436
  723.4 103.2 %copy-start.45 = (f32[256]{0:T(256)S(1)}, f32[256]{0:T(256)}, u32[]{:S(2)}) copy-start(f32[256]{0:T(256)} %get-tuple-element.113) | copy-start | bytes 3076
  (20 other events, 40.5 us)
Sparse Core Ops, SparseCore 0:
  9.6 30.7 all-gather.11
  41.9 27.4 all-gather.9
  70.9 45.4 all-gather.13
  117.8 44.6 all-gather.15
  163.9 80.4 all-gather.19
  245.8 79.3 all-gather.17
  326.8 79.0 all-gather.21
  670.4 23.5 reduce-scatter.18
  697.0 25.7 reduce-scatter.16
  725.6 42.4 reduce-scatter.14
  771.1 43.1 reduce-scatter.20
  817.0 18.3 reduce-scatter.22
  837.8 74.8 reduce-scatter.12
  914.9 77.2 reduce-scatter.8
  994.4 77.2 reduce-scatter.10
  1075.1 59.7 all-reduce.6
where the time goes:
time: 1160 us; the launch traced here: 1150 us
  waiting for transfers between devices  714 us (62%)
  matrix products  148 us (13%)
  local copies, waits for them, and re-layouts  118 us (10%)
  blocking collectives  67 us (6%)
  other arithmetic  65.8 us (6%)
  starting transfers between devices  21.7 us (2%)
  between operations  16 us (1%)
    reduce_scatter x1, waiting for transfers between devices, on_device(): lax.psum_scatter(gate_part.astype(jnp.bfloat16), 'dp', scatter_dimension=...  76.7 us
    reduce_scatter x1, waiting for transfers between devices, on_device(): lax.psum_scatter(up_part.astype(jnp.bfloat16), 'dp', scatter_dimension=1,...  76.7 us
    all_to_all x1, waiting for transfers between devices, on_device(): lax.all_to_all(entry_back, 'expert', split_axis=0, concat_axis=0, tiled=T...  73 us
    all_gather x1, waiting for transfers between devices, on_device(): lax.all_gather(expert_down, 'dp', axis=2, tiled=True)  68.4 us
    psum x1, waiting for transfers between devices, on_device(): lax.psum(query_part.astype(jnp.bfloat16), 'expert').astype(jnp.float32)  60.4 us
    all_to_all x1, waiting for transfers between devices, on_device(): lax.all_to_all(produced, 'expert', split_axis=0, concat_axis=0, tiled=True)  59.5 us
    reduce_scatter x1, waiting for transfers between devices, on_device(): lax.psum_scatter(down_part.astype(jnp.bfloat16), 'dp', scatter_dimension=...  52.6 us
    reduce_scatter x1, waiting for transfers between devices, on_device(): lax.psum_scatter(summed[3].astype(jnp.bfloat16), 'dp', scatter_dimension=...  46.2 us
  transfers between devices with their start and end apart: 20, of which 15 were waited for; matrix products, arithmetic and copies ran while one was open for 22% of the time, Pallas kernels for 0%

commit v1 on v0

v1 whole, which is shorter than its diff:
```python
import jax
import jax.numpy as jnp
from jax import lax
from jax.experimental import pallas as pl
from jax.experimental.pallas import tpu as pltpu
from jax.sharding import PartitionSpec as P

D = 1024
HEADS = 16
KV_HEADS = 8
HEAD_DIM = 64
EXPERTS = 32
TOPK = 8
CAP = 128
FF = 512
BLOCK = 256
EXTRA = 16
HELD = BLOCK + EXTRA
HD = HEADS * HEAD_DIM
KVD = KV_HEADS * HEAD_DIM

EPSILON = 1e-06
THETA = 10000.0
F32 = jnp.float32
BF16 = jnp.bfloat16

CORE, X_WAY, Y_WAY = 1, 2, 4


def layout_tables(length_row, count):
    places = jnp.arange(count, dtype=jnp.int32)
    ends = jnp.cumsum(length_row)
    passed = places[:, None] >= ends[None, :]
    begins = jnp.sum(jnp.where(passed, length_row[None, :], 0), axis=1)
    position = (places - begins).astype(F32)
    frequency = THETA ** (-(jnp.arange(HEAD_DIM // 2, dtype=F32) * 2.0 / HEAD_DIM))
    angles = position[:, None] * frequency[None, :]
    cosine = jnp.concatenate([jnp.cos(angles), jnp.cos(angles)], axis=-1)
    sine = jnp.concatenate([jnp.sin(angles), jnp.sin(angles)], axis=-1)
    return (cosine, sine)


def contract_rows(left, right):
    return lax.dot_general(left, right, (((0,), (0,)), ((), ())), preferred_element_type=F32)


def times_transpose(left, right):
    return lax.dot_general(left, right, (((1,), (1,)), ((), ())), preferred_element_type=F32)


def times(left, right):
    return jnp.dot(left, right, preferred_element_type=F32)


def rotate(values):
    width = values.shape[1]
    lane = lax.broadcasted_iota(jnp.int32, values.shape, 1)
    half = HEAD_DIM // 2
    return jnp.where(
        lax.rem(lane, HEAD_DIM) < half,
        -pltpu.roll(values, width - half, 1),
        pltpu.roll(values, half, 1),
    )


def wide(table, width):
    return jnp.concatenate([table] * (width // table.shape[1]), axis=1)


def allowed_pairs(length_ref, count):
    row = lax.broadcasted_iota(jnp.int32, (count, count), 0)
    column = lax.broadcasted_iota(jnp.int32, (count, count), 1)
    allowed = column <= row
    end = 0
    for s in range(length_ref.shape[0] - 1):
        end = end + length_ref[s]
        allowed = allowed & ((row >= end) == (column >= end))
    allowed = jnp.where(allowed, 1.0, 0.0)
    return jnp.concatenate([allowed, allowed], axis=0) > 0.0


def pair(value, h):
    at = 2 * HEAD_DIM * h
    return jnp.concatenate(
        [value[:, at : at + HEAD_DIM], value[:, at + HEAD_DIM : at + 2 * HEAD_DIM]], axis=0
    )


def beside(value):
    count = value.shape[0] // 2
    return jnp.concatenate([value[:count], value[count:]], axis=1)


def key_head(value, h):
    return value[:, HEAD_DIM * h : HEAD_DIM * (h + 1)]


def gains(dense_ref):
    lines = dense_ref[:, 3 * D :].astype(F32).T
    return lines[EXPERTS : EXPERTS + 1], lines[EXPERTS + 1 : EXPERTS + 2]


SCALE = HEAD_DIM ** (-0.5)
QKV = HD + 2 * KVD
WHOLE = pl.BlockSpec(memory_space=pltpu.VMEM)
SCALARS = pl.BlockSpec(memory_space=pltpu.SMEM)


def forward_call(lengths, tokens, dense, cosine, sine):
    count = tokens.shape[0]

    def body(
        length_ref, token_ref, dense_ref, cos_ref, sin_ref,
        n1_ref, q_ref, k_ref, v_ref, att_ref, lse_ref, res_ref, n2_ref, logit_ref,
    ):
        gain_a, gain_b = gains(dense_ref)
        x = token_ref[...].astype(F32)
        r1 = lax.rsqrt(jnp.mean(x * x, axis=1, keepdims=True) + EPSILON)
        n1 = (x * r1 * gain_a).astype(BF16)
        n1_ref[...] = n1
        qkv = times(n1, dense_ref[:, :QKV])
        q_lin, k_lin = qkv[:, :HD], qkv[:, HD : HD + KVD]
        cos, sin = wide(cos_ref[...], HD), wide(sin_ref[...], HD)
        q = ((q_lin * cos + rotate(q_lin) * sin) * SCALE).astype(BF16)
        k = (k_lin * cos[:, :KVD] + rotate(k_lin) * sin[:, :KVD]).astype(BF16)
        v = qkv[:, HD + KVD :].astype(BF16)
        q_ref[...], k_ref[...], v_ref[...] = q, k, v
        allowed = allowed_pairs(length_ref, count)
        lane = lax.broadcasted_iota(jnp.int32, (count, 128), 1)
        lse = jnp.zeros((count, 128), F32)
        for h in range(KV_HEADS):
            scores = times_transpose(pair(q, h), key_head(k, h))
            scores = jnp.where(allowed, scores, -1e30)
            highest = jnp.max(scores, axis=1, keepdims=True)
            raised = jnp.exp(scores - highest)
            total = jnp.sum(raised, axis=1, keepdims=True)
            probs = (raised / total).astype(BF16)
            mixed = times(probs, key_head(v, h))
            att_ref[:, 2 * HEAD_DIM * h : 2 * HEAD_DIM * (h + 1)] = beside(mixed).astype(BF16)
            logs = highest + jnp.log(total)
            lse = jnp.where(lane == 2 * h, logs[:count], lse)
            lse = jnp.where(lane == 2 * h + 1, logs[count:], lse)
        lse_ref[...] = lse
        residual = x + times(att_ref[...], dense_ref[:, QKV : QKV + D])
        res_ref[...] = residual
        r2 = lax.rsqrt(jnp.mean(residual * residual, axis=1, keepdims=True) + EPSILON)
        n2 = (residual * r2 * gain_b).astype(BF16)
        n2_ref[...] = n2
        logit_ref[...] = times(n2, dense_ref[:, 3 * D :])

    def out(width, dtype):
        return jax.ShapeDtypeStruct((count, width), dtype)

    return pl.pallas_call(
        body,
        in_specs=[SCALARS] + [WHOLE] * 4,
        out_specs=[WHOLE] * 9,
        out_shape=[
            out(D, BF16), out(HD, BF16), out(KVD, BF16), out(KVD, BF16), out(HD, BF16),
            out(128, F32), out(D, F32), out(D, BF16), out(128, F32),
        ],
        compiler_params=pltpu.CompilerParams(vmem_limit_bytes=56 * 1024 * 1024),
        cost_estimate=pl.CostEstimate(flops=50 * 10**9, bytes_accessed=10**7, transcendentals=0),
        name="attention_forward",
    )(lengths, tokens, dense, cosine, sine)


def backward_call(lengths, tokens, cotangent, dense, cosine, sine, kept, logit_back, back_rows):
    count = tokens.shape[0]

    def body(
        length_ref, token_ref, dy_ref, dense_ref, cos_ref, sin_ref,
        n1_ref, q_ref, k_ref, v_ref, att_ref, lse_ref, res_ref, n2_ref, lb_ref, back_ref,
        input_ref, late_ref, early_ref,
    ):
        gain_a, gain_b = gains(dense_ref)
        residual = res_ref[...]
        r2 = lax.rsqrt(jnp.mean(residual * residual, axis=1, keepdims=True) + EPSILON)
        back = times_transpose(lb_ref[...], dense_ref[:, 3 * D :]) + back_ref[...]
        second_terms = (back * residual * r2).astype(BF16)
        scaled = back * gain_b
        residual_back = (
            dy_ref[...].astype(F32)
            + r2 * scaled
            - residual * (r2 * r2 * r2) * jnp.mean(scaled * residual, axis=1, keepdims=True)
        )
        branch_back = residual_back.astype(BF16)
        early_ref[...] = contract_rows(att_ref[...], branch_back).astype(BF16)
        att_back = times_transpose(branch_back, dense_ref[:, QKV : QKV + D]).astype(BF16)
        q, k, v, lse = q_ref[...], k_ref[...], v_ref[...], lse_ref[...]
        allowed = allowed_pairs(length_ref, count)
        q_back, k_back, v_back = [], [], []
        for h in range(KV_HEADS):
            queries, keys, values = pair(q, h), key_head(k, h), key_head(v, h)
            grads = pair(att_back, h)
            logs = jnp.concatenate([lse[:, 2 * h : 2 * h + 1], lse[:, 2 * h + 1 : 2 * h + 2]], axis=0)
            scores = jnp.where(allowed, times_transpose(queries, keys), -1e30)
            probs = jnp.exp(scores - logs)
            prob_back = times_transpose(grads, values)
            spread = jnp.sum(prob_back * probs, axis=1, keepdims=True)
            score_back = (probs * (prob_back - spread)).astype(BF16)
            q_back.append(beside(times(score_back, keys)))
            k_back.append(contract_rows(score_back, queries))
            v_back.append(contract_rows(probs.astype(BF16), grads))
        q_back = jnp.concatenate(q_back, axis=1)
        k_back = jnp.concatenate(k_back, axis=1)
        v_back = jnp.concatenate(v_back, axis=1)
        cos, sin = wide(cos_ref[...], HD), wide(sin_ref[...], HD)
        q_back = ((q_back * cos - rotate(q_back * sin)) * SCALE).astype(BF16)
        k_back = (k_back * cos[:, :KVD] - rotate(k_back * sin[:, :KVD])).astype(BF16)
        qkv_back = jnp.concatenate([q_back, k_back, v_back.astype(BF16)], axis=1)
        late_ref[:, :QKV] = contract_rows(n1_ref[...], qkv_back).astype(BF16)
        first_back = times_transpose(qkv_back, dense_ref[:, :QKV])
        x = token_ref[...].astype(F32)
        r1 = lax.rsqrt(jnp.mean(x * x, axis=1, keepdims=True) + EPSILON)
        first_terms = (first_back * x * r1).astype(BF16)
        scaled = first_back * gain_a
        input_ref[...] = (
            residual_back
            + r1 * scaled
            - x * (r1 * r1 * r1) * jnp.mean(scaled * x, axis=1, keepdims=True)
        )
        lane = lax.broadcasted_iota(jnp.int32, (count, 128), 1)
        marks = [jnp.where(lane == EXPERTS + s, 1.0, 0.0).astype(BF16) for s in (0, 1)]
        late_ref[:, QKV:] = (
            contract_rows(n2_ref[...], lb_ref[...])
            + contract_rows(first_terms, marks[0])
            + contract_rows(second_terms, marks[1])
        ).astype(BF16)

    return pl.pallas_call(
        body,
        in_specs=[SCALARS] + [WHOLE] * 15,
        out_specs=[WHOLE] * 3,
        out_shape=[
            jax.ShapeDtypeStruct((count, D), F32),
            jax.ShapeDtypeStruct((D, QKV + 128), BF16),
            jax.ShapeDtypeStruct((D, D), BF16),
        ],
        compiler_params=pltpu.CompilerParams(vmem_limit_bytes=56 * 1024 * 1024),
        cost_estimate=pl.CostEstimate(flops=50 * 10**9, bytes_accessed=10**7, transcendentals=0),
        name="attention_backward",
    )(lengths, tokens, cotangent, dense, cosine, sine, *kept[:8], logit_back, back_rows)


def swap(value, axis, mask):
    size = lax.axis_size(axis)
    return lax.ppermute(value, axis, [(k, k ^ mask) for k in range(size)])


def tie(value, *first):
    return lax.optimization_barrier((value, first))[0]


def pack_weights(gate, up, down):
    rows = gate.shape[1]
    parts = [down[:, at : at + rows] for at in range(0, FF, rows)]
    return jnp.concatenate([gate, up] + parts, axis=2)


def expert_call(expert, rows, grads, weights, shards, before):
    steps = rows[0].shape[0] // HELD
    chained = before is not None
    size = D // shards
    squares = [(s, q) for s in range(shards) for q in range(FF // size)]

    def body(expert_ref, *refs):
        row_refs, grad_refs, weight_ref = refs[0:4], refs[4:8], refs[8]
        at = 9
        if chained:
            mix_before, back_before = refs[9:13], refs[13:17]
            at = 17
        mix_refs, back_refs = refs[at : at + 4], refs[at + 4 : at + 8]
        weight_grad_ref, down, gu_total, down_total = refs[at + 8 :]
        step = pl.program_id(0)

        @pl.when(step == 0)
        def _():
            gu_total[...] = jnp.zeros_like(gu_total)
            down_total[...] = jnp.zeros_like(down_total)
            for s, q in squares:
                down[q * size : (q + 1) * size, s * size : (s + 1) * size] = weight_ref[
                    s * size : (s + 1) * size, 2 * FF + q * size : 2 * FF + (q + 1) * size
                ]

        def by_token(value):
            value = value[0:1] + value[1:2]
            return sum(value[:, at : at + BLOCK] for at in range(0, D, BLOCK))

        counts, gate_lines = [], []
        for b in range(4):
            named = grad_refs[b][BLOCK:, :].astype(F32)[0:2] == expert_ref[0].astype(F32)
            gates = row_refs[b][BLOCK:, :].astype(F32)
            gates = gates[0:2] + gates[2:4]
            counts.append(by_token(jnp.where(named, 1.0, 0.0)))
            gate_lines.append(by_token(jnp.where(named, gates, 0.0)))
        hit = jnp.concatenate(counts + [jnp.zeros((4, BLOCK), F32)], axis=0)
        earlier = lax.broadcasted_iota(jnp.int32, (BLOCK, BLOCK), 0) < lax.broadcasted_iota(
            jnp.int32, (BLOCK, BLOCK), 1
        )
        slots = times(hit.astype(BF16), jnp.where(earlier, 1.0, 0.0).astype(BF16))
        slots = jnp.where(hit > 0.0, slots, -1.0).astype(jnp.int32)
        slot_ids = lax.broadcasted_iota(jnp.int32, (CAP, BLOCK), 0)
        hots, hots_low, z, raw, gate_cols = [], [], [], [], []
        for b in range(4):
            hot = slots[b : b + 1] == slot_ids
            hot_low = jnp.where(hot, 1.0, 0.0).astype(BF16)
            z.append(times(hot_low, row_refs[b][:BLOCK, :]).astype(BF16))
            raw.append(times(hot_low, grad_refs[b][:BLOCK, :]))
            gate_cols.append(
                jnp.sum(jnp.where(hot, gate_lines[b], 0.0), axis=1, keepdims=True)
            )
            hots.append(hot)
            hots_low.append(hot_low)
        z = jnp.concatenate(z, axis=0)
        raw = jnp.concatenate(raw, axis=0)
        gate_col = jnp.concatenate(gate_cols, axis=0)
        both = times(z, weight_ref[:, : 2 * FF])
        gate_pre, up_pre = both[:, :FF], both[:, FF:]
        sigma = jax.nn.sigmoid(gate_pre)
        activated = gate_pre * sigma
        hidden = (activated * up_pre).astype(BF16)
        produced = times(hidden, down[...]).astype(BF16).astype(F32)
        gate_back = jnp.sum(raw * produced, axis=1, keepdims=True)
        weighted = (gate_col * produced).astype(BF16)
        slot_back = (gate_col * raw).astype(BF16)
        hidden_back = times_transpose(slot_back, down[...])
        gate_slope = (hidden_back * up_pre * sigma * (1.0 + gate_pre * (1.0 - sigma))).astype(BF16)
        up_slope = (hidden_back * activated).astype(BF16)
        slopes = jnp.concatenate([gate_slope, up_slope], axis=1)
        gu_total[...] += contract_rows(z, slopes)
        down_total[...] += contract_rows(hidden, slot_back)
        entry_back = times_transpose(slopes, weight_ref[:, : 2 * FF]).astype(BF16)
        ranks = lax.broadcasted_iota(jnp.int32, (EXPERTS // 4, BLOCK), 0)
        for b in range(4):
            part = slice(b * CAP, (b + 1) * CAP)
            mixed = contract_rows(hots_low[b], weighted[part])
            back = contract_rows(hots_low[b], entry_back[part])
            line = jnp.sum(jnp.where(hots[b], gate_back[part], 0.0), axis=0, keepdims=True)
            extra = jnp.concatenate(
                [jnp.where(ranks * 4 + q == expert_ref[0], line, 0.0) for q in range(4)], axis=1
            )
            high = extra.astype(BF16).astype(F32)
            extra = jnp.concatenate([high, extra - high], axis=0)
            if chained:
                mixed = mixed + mix_before[b][:BLOCK, :].astype(F32)
                back = back + back_before[b][:BLOCK, :].astype(F32)
                extra = extra + back_before[b][BLOCK:, :].astype(F32)
            mix_refs[b][:BLOCK, :] = mixed.astype(BF16)
            mix_refs[b][BLOCK:, :] = jnp.zeros((EXTRA, D), BF16)
            back_refs[b][:BLOCK, :] = back.astype(BF16)
            back_refs[b][BLOCK:, :] = extra.astype(BF16)

        @pl.when(step == steps - 1)
        def _():
            weight_grad_ref[:, : 2 * FF] = gu_total[...].astype(BF16)
            for s, q in squares:
                weight_grad_ref[
                    s * size : (s + 1) * size, 2 * FF + q * size : 2 * FF + (q + 1) * size
                ] = down_total[q * size : (q + 1) * size, s * size : (s + 1) * size].astype(BF16)

    row_spec = pl.BlockSpec((HELD, D), lambda s: (s, 0))
    weight_spec = pl.BlockSpec((D, 3 * FF), lambda s: (0, 0), pipeline_mode=pl.Buffered(1))
    rows_shape = jax.ShapeDtypeStruct(rows[0].shape, BF16)
    extra = list(before[0]) + list(before[1]) if chained else []
    outs = pl.pallas_call(
        body,
        grid=(steps,),
        in_specs=[pl.BlockSpec(memory_space=pltpu.SMEM)]
        + [row_spec] * 8
        + [weight_spec]
        + [row_spec] * len(extra),
        out_specs=[row_spec] * 8 + [weight_spec],
        out_shape=[rows_shape] * 8
        + [jax.ShapeDtypeStruct((D, 3 * FF), BF16)],
        scratch_shapes=[
            pltpu.VMEM((FF, D), BF16),
            pltpu.VMEM((D, 2 * FF), F32),
            pltpu.VMEM((FF, D), F32),
        ],
        compiler_params=pltpu.CompilerParams(vmem_limit_bytes=60 * 1024 * 1024),
        cost_estimate=pl.CostEstimate(flops=1000, bytes_accessed=1000, transcendentals=0),
        name="experts",
    )(expert, *rows, *grads, weights, *extra)
    return outs[0:4], outs[4:8], outs[8]


def with_extra(block, low):
    count = TOPK * BLOCK // D
    lines = [part.reshape(count, D).astype(BF16) for part in low]
    lines.append(jnp.zeros((EXTRA - count * len(low), D), BF16))
    return jnp.concatenate([block] + lines, axis=0)


class Cube:
    HALF = 144

    def __init__(self, experts_here):
        self.place = lax.axis_index("expert")
        self.line = lax.axis_index("dp")
        self.odd = lax.rem(self.line, 2)
        self.share = experts_here // 2
        self.shards = 4
        self.own_ids = experts_here * self.place + self.share * self.odd + jnp.arange(self.share)

    def spread(self, block):
        first, second = block[: self.HALF], block[self.HALF :]
        first_x = swap(first, "expert", X_WAY)
        second_y = swap(second, "expert", Y_WAY)
        first_y = swap(jnp.concatenate([first, first_x]), "expert", Y_WAY)
        second_x = swap(jnp.concatenate([second, second_y]), "expert", X_WAY)
        return first, second, first_x, second_x, first_y, second_y

    def join(self, pieces):
        first, second, first_x, second_x, first_y, second_y = pieces
        rest = HELD - self.HALF
        return jnp.concatenate(
            [
                first,
                second,
                first_x,
                second_x[:rest],
                first_y[: self.HALF],
                second_y,
                first_y[self.HALF :],
                second_x[rest:],
            ],
            axis=0,
        )

    def cross(self, block):
        return swap(block, "dp", 1)

    def both_cores(self, near, far):
        near, far = self.join(near), self.join(far)
        return [near, swap(near, "expert", CORE), far, swap(far, "expert", CORE)]


    def fold_cores(self, parts):
        near, near_other, far, far_other = parts
        far = (far.astype(F32) + swap(far_other, "expert", CORE).astype(F32)).astype(BF16)
        near = (near.astype(F32) + swap(near_other, "expert", CORE).astype(F32)).astype(BF16)
        return far, near

    def fold_once(self, parts):
        folded = []
        for part in parts:
            part = part.reshape(2, 2, HELD, D)
            first, second = part[:, :, : self.HALF], part[:, :, self.HALF :]
            first = first[0].astype(F32) + swap(first[1], "expert", Y_WAY).astype(F32)
            second = second[:, 0].astype(F32) + swap(second[:, 1], "expert", X_WAY).astype(F32)
            folded.append((first.astype(BF16), second.astype(BF16)))
        return folded

    def fold_twice(self, folded):
        blocks = []
        for first, second in folded:
            first = first[0].astype(F32) + swap(first[1], "expert", X_WAY).astype(F32)
            second = second[0].astype(F32) + swap(second[1], "expert", Y_WAY).astype(F32)
            blocks.append(jnp.concatenate([first, second], axis=0).astype(BF16))
        return blocks

    def fold_planes(self, blocks):
        far, near = blocks
        return near.astype(F32) + swap(far, "dp", 1).astype(F32)

    def weight(self, shards, e):
        low, high = shards[e], shards[self.share + e]
        sent = jnp.stack([low, high, low, high])
        whole = lax.all_to_all(sent, "dp", split_axis=0, concat_axis=0, tiled=True)
        return whole.reshape(D, 3 * FF)

    def weight_grad(self, total):
        parts = total.reshape(4, D // 4, 3 * FF)
        return lax.all_to_all(parts, "dp", split_axis=0, concat_axis=0, tiled=True)

    def weight_grads(self, arrived):
        low = [got[0].astype(F32) + got[2].astype(F32) for got in arrived]
        high = [got[1].astype(F32) + got[3].astype(F32) for got in arrived]
        return jnp.stack(low + high)

    def gather_dense(self, shard):
        part, width = shard.shape[0] // 8, shard.shape[1]
        middle = width // 256 * 128
        own = lax.dynamic_slice_in_dim(shard, self.place * part, part, 0)[None, None]
        lines = jnp.zeros((4, 1, part, width), shard.dtype)
        for mask in range(4):
            piece = swap(own, "dp", mask) if mask else own
            lines = lax.dynamic_update_slice(lines, piece, (self.line ^ mask, 0, 0, 0))
        first, second = lines[..., :middle], lines[..., middle:]
        first_x = swap(first, "expert", X_WAY)
        second_y = swap(second, "expert", Y_WAY)
        firsts = swap(jnp.concatenate([first, first_x], axis=1), "expert", Y_WAY)
        seconds = swap(jnp.concatenate([second, second_y], axis=1), "expert", X_WAY)
        found = (
            (lines, 0, 0, (0,)),
            (first_x, X_WAY, 0, (0,)),
            (second_y, Y_WAY, middle, (0,)),
            (firsts, Y_WAY, 0, (0, X_WAY)),
            (seconds, X_WAY, middle, (0, Y_WAY)),
        )
        whole = jnp.zeros((4, 8, part, width), shard.dtype)
        for pieces, mask, at, more in found:
            other = swap(pieces, "expert", CORE)
            for k, bits in enumerate(more):
                where = self.place ^ (mask | bits)
                whole = lax.dynamic_update_slice(whole, pieces[:, k : k + 1], (0, where, 0, at))
                where = where ^ CORE
                whole = lax.dynamic_update_slice(whole, other[:, k : k + 1], (0, where, 0, at))
        return whole.reshape(-1, width), lines


    def fold_dense(self, totals):
        core, x, y = [lax.rem(lax.div(self.place, way), 2) for way in (CORE, X_WAY, Y_WAY)]

        def fold(value, bit, axis, mask):
            kept = lax.dynamic_index_in_dim(value, bit, axis, keepdims=False)
            sent = lax.dynamic_index_in_dim(value, 1 - bit, axis, keepdims=False)
            return (kept.astype(F32) + swap(sent, "expert", mask).astype(F32)).astype(BF16)

        found = []
        for total, x_first in zip(totals, (False, True)):
            width, part = total.shape[1], total.shape[0] // 32
            lines = fold(total.reshape(4, 2, 2, 2, part, width), core, 3, CORE)
            if x_first:
                found.append(fold(fold(lines, x, 2, X_WAY), y, 1, Y_WAY))
            else:
                found.append(fold(fold(lines, y, 1, Y_WAY), x, 1, X_WAY))
        return found

    def sum_dense(self, found):
        sums = []
        for lines in found:
            summed = lax.dynamic_index_in_dim(lines, self.line, 0).astype(F32)
            for mask in (1, 2, 3):
                sent = lax.dynamic_index_in_dim(lines, self.line ^ mask, 0)
                summed = summed + swap(sent, "dp", mask).astype(F32)
            sums.append(summed.astype(BF16))
        return sums

    def spread_dense(self, sums):
        found = []
        for summed in sums:
            _, part, width = summed.shape
            whole = jnp.zeros((8, part, width), BF16)
            for mask in range(8):
                piece = swap(summed, "expert", mask) if mask else summed
                whole = lax.dynamic_update_slice(whole, piece, (self.place ^ mask, 0, 0))
            found.append(whole.reshape(-1, width).astype(F32))
        return found


class Plain:
    def __init__(self, experts_here):
        self.share = experts_here
        self.shards = lax.axis_size("dp")
        self.own_ids = experts_here * lax.axis_index("expert") + jnp.arange(experts_here)

    def spread(self, block):
        return block

    def cross(self, block):
        return block

    def both_cores(self, near, far):
        whole = lax.all_gather(near, "expert", axis=0, tiled=True)
        return jnp.split(whole, 4, axis=0)

    def fold_cores(self, parts):
        whole = jnp.concatenate(parts, axis=0)
        return [lax.psum_scatter(whole, "expert", scatter_dimension=0, tiled=True)]

    def fold_once(self, parts):
        return parts

    def fold_twice(self, parts):
        return parts

    def fold_planes(self, blocks):
        return blocks[0].astype(F32)

    def gather_dense(self, shard):
        part = shard.shape[0] // lax.axis_size("expert")
        own = lax.dynamic_slice_in_dim(shard, lax.axis_index("expert") * part, part, 0)
        return lax.all_gather(own, ("dp", "expert"), axis=0, tiled=True), own

    def weight(self, shards, e):
        return lax.all_gather(shards[e], "dp", axis=0, tiled=True)

    def weight_grad(self, total):
        return lax.psum_scatter(total, "dp", scatter_dimension=0, tiled=True)

    def weight_grads(self, arrived):
        return jnp.stack(arrived).astype(F32)

    def fold_dense(self, totals):
        both = ("dp", "expert")
        return [lax.psum_scatter(t, both, scatter_dimension=0, tiled=True) for t in totals]

    def sum_dense(self, sums):
        return sums

    def spread_dense(self, sums):
        return [lax.all_gather(t, "expert", axis=0, tiled=True).astype(F32) for t in sums]


def on_device(
    tokens,
    routes,
    lengths,
    query_weight,
    key_weight,
    value_weight,
    output_weight,
    router_weight,
    first_gain,
    second_gain,
    expert_gate,
    expert_up,
    expert_down,
    cotangent,
):
    tok_count = tokens.shape[0]
    here = expert_gate.shape[0]
    cube = lax.axis_size("dp") == 4 and lax.axis_size("expert") == 8 and here % 2 == 0
    plan = Cube(here) if cube else Plain(here)

    small = jnp.concatenate(
        [
            router_weight,
            first_gain[:, None],
            second_gain[:, None],
            jnp.zeros((router_weight.shape[0], 128 - EXPERTS - 2), BF16),
        ],
        axis=1,
    )
    grad_block = with_extra(cotangent, [routes.T.astype(F32)])
    grad_near = plan.spread(grad_block)
    dense, lines = plan.gather_dense(
        jnp.concatenate([query_weight, key_weight, value_weight, output_weight, small], axis=1)
    )
    grad_across = plan.cross(tie(grad_block, lines))
    grad_far = plan.spread(tie(grad_across, dense))
    shards = pack_weights(expert_gate, expert_up, expert_down)
    weights = [plan.weight(tie(shards, grad_across), 0)]

    cosine, sine = layout_tables(lengths[0], tok_count)
    cosine, sine = jnp.concatenate([cosine, cosine], axis=1), jnp.concatenate([sine, sine], axis=1)
    kept = forward_call(lengths[0], tokens, dense, cosine, sine)
    residual, normed_two, logits = kept[6:]
    logits = logits[:, :EXPERTS]
    choose = (routes[:, :, None] == jnp.arange(EXPERTS, dtype=jnp.int32)[None, None, :]).astype(F32)
    chosen = jnp.sum(choose * logits[:, None, :], axis=-1)
    top_chosen = jnp.max(chosen, axis=-1, keepdims=True)
    raised_gates = jnp.exp(chosen - top_chosen)
    gates = raised_gates / jnp.sum(raised_gates, axis=-1, keepdims=True)

    gate_lines = gates.T
    gate_high = lax.optimization_barrier(gate_lines.astype(BF16))
    gate_low = gate_lines - gate_high.astype(F32)
    block, grad_far = lax.optimization_barrier(
        (with_extra(normed_two, [gate_high, gate_low]), grad_far)
    )
    rows_across = plan.cross(block)
    rows = plan.both_cores(plan.spread(block), plan.spread(rows_across))
    grad_rows = plan.both_cores(grad_near, grad_far)
    for e in range(1, plan.share):
        weights.append(plan.weight(tie(shards, rows_across, weights[-1]), e))

    done, weight_parts = None, []
    for e in range(plan.share):
        mixes, backs, weight_part = expert_call(
            plan.own_ids[e : e + 1].astype(jnp.int32),
            rows,
            grad_rows,
            weights[e],
            plan.shards,
            done,
        )
        done = (mixes, backs)
        weight_parts.append(weight_part)

    arrived = [plan.weight_grad(weight_parts[0])]
    folded = plan.fold_once(plan.fold_cores(done[1]))
    mixes = plan.fold_once(plan.fold_cores(done[0]))
    folded, mixes, arrived = lax.optimization_barrier((folded, mixes, arrived))
    back_held = plan.fold_planes(plan.fold_twice(folded))
    back_rows = back_held[:BLOCK]
    owners_back = back_held[BLOCK : BLOCK + EXTRA // 2] + back_held[BLOCK + EXTRA // 2 :]
    owners_back = owners_back.reshape(EXPERTS, BLOCK)
    for part in weight_parts[1:]:
        arrived.append(plan.weight_grad(tie(part, back_rows)))
    mixes = plan.fold_twice(tie(mixes, back_rows))

    gate_back = jnp.sum(choose * owners_back.T[:, None, :], axis=-1)
    chosen_back = gates * (gate_back - jnp.sum(gates * gate_back, axis=-1, keepdims=True))
    logit_back = jnp.sum(chosen_back[:, :, None] * choose, axis=1).astype(BF16)
    logit_back = jnp.pad(logit_back, ((0, 0), (0, 128 - EXPERTS)))
    input_grad, late, early = backward_call(
        lengths[0], tokens, cotangent, dense, cosine, sine, kept, logit_back, back_rows
    )
    late, early, mixes = lax.optimization_barrier((late, early, mixes))
    sums, arrived = lax.optimization_barrier((plan.fold_dense([late, early]), arrived))
    mixture = plan.fold_planes(tie(mixes, sums))
    output = (residual + mixture[:BLOCK]).astype(BF16)
    late, early = plan.spread_dense(plan.sum_dense(sums))
    weight_grad = plan.weight_grads(arrived)
    return (
        output,
        input_grad,
        late[:, :HD],
        late[:, HD : HD + KVD],
        late[:, HD + KVD : HD + 2 * KVD],
        early,
        late[:, HD + 2 * KVD : HD + 2 * KVD + EXPERTS],
        late[:, HD + 2 * KVD + EXPERTS],
        late[:, HD + 2 * KVD + EXPERTS + 1],
        weight_grad[:, :, :FF],
        weight_grad[:, :, FF : 2 * FF],
        jnp.concatenate(
            jnp.split(weight_grad[:, :, 2 * FF :], FF // weight_grad.shape[1], axis=2), axis=1
        ),
    )


def solution(mesh):
    return jax.shard_map(
        on_device,
        mesh=mesh,
        in_specs=(
            P(("dp", "expert"), None),
            P(("dp", "expert"), None),
            P(("dp", "expert"), None),
            P("dp", None),
            P("dp", None),
            P("dp", None),
            P("dp", None),
            P("dp", None),
            P("dp"),
            P("dp"),
            P("expert", "dp", None),
            P("expert", "dp", None),
            P("expert", None, "dp"),
            P(("dp", "expert"), None),
        ),
        out_specs=(
            P(("dp", "expert"), None),
            P(("dp", "expert"), None),
            P("dp", None),
            P("dp", None),
            P("dp", None),
            P("dp", None),
            P("dp", None),
            P("dp"),
            P("dp"),
            P("expert", "dp", None),
            P("expert", "dp", None),
            P("expert", None, "dp"),
        ),
        check_vma=False,
    )
```

time: 1160 us -> 569 us (0.49)
  waiting for transfers between devices: 714 us -> 179 us
  matrix products: 148 us -> 0 us
  Pallas kernels: 0 us -> 109 us
  starting transfers between devices: 21.7 us -> 100 us
  blocking collectives: 67 us -> 0 us
  between operations: 16 us -> 1.96 us
    reduce_scatter x8 -> x0, waiting for transfers between devices: 302 us -> none  [the longest x1 76.7 us: on_device(): lax.psum_scatter(gate_part.astype(jnp.bfloat16), 'dp', scatter_dimension=...]
    all_gather x7 -> x0, waiting for transfers between devices: 171 us -> none  [the longest x1 68.4 us: on_device(): lax.all_gather(expert_down, 'dp', axis=2, tiled=True)]
    ppermute x0 -> x82, waiting for transfers between devices: none -> 150 us  [swap(): return lax.ppermute(value, axis, [(k, k ^ mask) for k in range(size)])]
    dot_general x30 -> x0, matrix products: 148 us -> none  [the longest x1 16.7 us: on_device(): jnp.einsum('sjcd,jfd->sjcf', grads_in, full_down, preferred_element_type=...]
    all_to_all x4, waiting for transfers between devices: 175 us -> 28.9 us  [the longest x2 28.9 us: weight_grad(): return lax.all_to_all(parts, 'dp', split_axis=0, concat_axis=0, tiled=True)]
    pallas_call x0 -> x4, Pallas kernels: none -> 109 us  [the longest x2 77.7 us: expert_call(): pl.pallas_call(body, grid=(steps,), in_specs=[pl.BlockSpec(memory_space=p...]
    ppermute x0 -> x82, starting transfers between devices: none -> 82.4 us  [swap(): return lax.ppermute(value, axis, [(k, k ^ mask) for k in range(size)])]
    gather x4 -> x0, local copies, waits for them, and re-layouts: 68 us -> none  [the longest x1 18.6 us: on_device(): upstream[holder]]
  transfers between devices with their start and end apart: 20 -> 86, of which waited for: 15 -> 35; matrix products, arithmetic and copies ran while one was open for 22% -> 26% of each run, Pallas kernels for 0% -> 12%
where the time goes in v1:
time: 569 us; the launch traced here: 562 us
  waiting for transfers between devices  179 us (31%)
  local copies, waits for them, and re-layouts  109 us (19%)
  Pallas kernels  109 us (19%)
  starting transfers between devices  100 us (18%)
  other arithmetic  63.5 us (11%)
    ppermute x82, waiting for transfers between devices, swap(): return lax.ppermute(value, axis, [(k, k ^ mask) for k in range(size)])  150 us
    ppermute x82, starting transfers between devices, swap(): return lax.ppermute(value, axis, [(k, k ^ mask) for k in range(size)])  82.4 us
    pallas_call x2, Pallas kernels, expert_call(): pl.pallas_call(body, grid=(steps,), in_specs=[pl.BlockSpec(memory_space=p...  77.7 us
    unnamed x86, local copies, waits for them, and re-layouts  40.2 us
    all_to_all x2, waiting for transfers between devices, weight_grad(): return lax.all_to_all(parts, 'dp', split_axis=0, concat_axis=0, tiled=True)  28.9 us
    pallas_call x1, Pallas kernels, backward_call(): pl.pallas_call(body, in_specs=[SCALARS] + [WHOLE] * 15, out_specs=[WHOLE]...  19 us
    pallas_call x1, Pallas kernels, forward_call(): pl.pallas_call(body, in_specs=[SCALARS] + [WHOLE] * 4, out_specs=[WHOLE]...  12 us
  transfers between devices with their start and end apart: 86, of which 35 were waited for; matrix products, arithmetic and copies ran while one was open for 26% of the time, Pallas kernels for 12%

profile of v1, /device:TPU:0, one launch (start us, length us, event | category | flops | bytes accessed | tf_op | source)
XLA Modules:
  0.0 562.5 jit_solution(2553628178737174468)
XLA Ops:
  3.1 2.6 concatenate.83
  7.4 3.0 collective-permute-start
  10.4 2.6 collective-permute-start.1
  24.3 4.1 collective-permute-done.1
  36.8 3.2 broadcast_in_dim.54
  54.0 2.8 collective-permute-done.12
  59.6 4.9 all-to-all-start
  78.7 3.1 collective-permute-done.8
  94.1 12.0 %attention_forward.1 = (bf16[256,1024]{1,0:T(8,128)(2,1)}, bf16[256,1024]{1,0:T(8,128)(2,1)}, bf16[256,512]{1,0:T(8,128)(2,1)}, bf16[256,512]{1,0:T(8,128)(2,1)}...) custom-call(s32[4]{0:T(128)} %bitcast.201, ...), custom_call_target="tpu_custom_call" | custom-call | flops 49999998976 | bytes 10000000 | tf_op jit(solution)/shard_map/attention_forward/pallas_call | solution.py:154
  111.2 6.0 %collective-permute-done.13 = bf16[144,1024]{1,0:T(8,128)(2,1)} collective-permute-done((bf16[144,1024]{1,0:T(8,128)(2,1)S(1)}, bf16[144,1024]{1,0:T(8,128)(2,1)}, u32[]{:S(2)}, u32[]{:S(2)}) %collective-permute-start.13) | collective-permute-done | bytes 294944 | tf_op jit(solution)/shard_map/ppermute | solution.py:248
  121.7 6.0 %collective-permute-done.15 = bf16[256,1024]{1,0:T(8,128)(2,1)} collective-permute-done((bf16[256,1024]{1,0:T(8,128)(2,1)}, bf16[256,1024]{1,0:T(8,128)(2,1)}, u32[]{:S(2)}, u32[]{:S(2)}) %collective-permute-start.15) | collective-permute-done | bytes 524320 | tf_op jit(solution)/shard_map/ppermute | solution.py:248
  127.7 5.5 collective-permute-done.16
  160.1 4.1 all-to-all-start.1
  169.2 5.9 %collective-permute-done.24 = bf16[128,1024]{1,0:T(8,128)(2,1)} collective-permute-done((bf16[128,1024]{1,0:T(8,128)(2,1)}, bf16[128,1024]{1,0:T(8,128)(2,1)}, u32[]{:S(2)}, u32[]{:S(2)}) %collective-permute-start.24) | collective-permute-done | bytes 262176 | tf_op jit(solution)/shard_map/ppermute | solution.py:248
  183.9 5.6 collective-permute-done.25
  195.7 4.1 collective-permute-done.27.refs_3_
  199.8 38.5 %experts.2 = (bf16[1088,1024]{1,0:T(8,128)(2,1)}, bf16[1088,1024]{1,0:T(8,128)(2,1)}, bf16[1088,1024]{1,0:T(8,128)(2,1)}, bf16[1088,1024]{1,0:T(8,128)(2,1)}, bf...) custom-call(s32[1]{0:T(128)} %get-tuple-element.238.expert_ref, ...), custom_call_target="tpu_custom_call" | custom-call | flops 1000 | bytes 1000 | tf_op jit(solution)/shard_map/experts/pallas_call | solution.py:366
  240.0 39.3 %experts.3 = (bf16[1088,1024]{1,0:T(8,128)(2,1)}, bf16[1088,1024]{1,0:T(8,128)(2,1)}, bf16[1088,1024]{1,0:T(8,128)(2,1)}, bf16[1088,1024]{1,0:T(8,128)(2,1)}, bf...) custom-call(s32[1]{0:T(128)} %get-tuple-element.239.expert_ref, ...), custom_call_target="tpu_custom_call" | custom-call | flops 1000 | bytes 1000 | tf_op jit(solution)/shard_map/experts/pallas_call | solution.py:366
  279.9 3.9 all-to-all-start.2
  284.3 3.5 add_convert_fusion.3
  287.8 2.7 add_convert_fusion.2
  298.7 7.4 %collective-permute-done.36 = bf16[2,128,1024]{2,1,0:T(8,128)(2,1)S(1)} collective-permute-done((bf16[2,128,1024]{2,1,0:T(8,128)(2,1)S(1)}, bf16[2,128,1024]{2,1,0:T(8,128)(2,1)S(1)}, u32[]{:S(2)}, u32[]{:S(2)}) %collective-permute-start.36) | collective-permute-done | bytes 524320 | tf_op jit(solution)/shard_map/ppermute | solution.py:248
  308.5 8.7 %collective-permute-done.39 = bf16[2,128,1024]{2,1,0:T(8,128)(2,1)S(1)} collective-permute-done((bf16[2,128,1024]{2,1,0:T(8,128)(2,1)S(1)}, bf16[2,128,1024]{2,1,0:T(8,128)(2,1)S(1)}, u32[]{:S(2)}, u32[]{:S(2)}) %collective-permute-start.39) | collective-permute-done | bytes 524320 | tf_op jit(solution)/shard_map/ppermute | solution.py:248
  319.8 8.7 %collective-permute-done.42 = bf16[2,128,1024]{2,1,0:T(8,128)(2,1)S(1)} collective-permute-done((bf16[2,128,1024]{2,1,0:T(8,128)(2,1)S(1)}, bf16[2,128,1024]{2,1,0:T(8,128)(2,1)S(1)}, u32[]{:S(2)}, u32[]{:S(2)}) %collective-permute-start.42) | collective-permute-done | bytes 524320 | tf_op jit(solution)/shard_map/ppermute | solution.py:248
  331.1 7.5 %collective-permute-done.45 = bf16[2,128,1024]{2,1,0:T(8,128)(2,1)S(1)} collective-permute-done((bf16[2,128,1024]{2,1,0:T(8,128)(2,1)S(1)}, bf16[2,128,1024]{2,1,0:T(8,128)(2,1)S(1)}, u32[]{:S(2)}, u32[]{:S(2)}) %collective-permute-start.45) | collective-permute-done | bytes 524320 | tf_op jit(solution)/shard_map/ppermute | solution.py:248
  345.1 9.7 %all-to-all-done.2 = bf16[4,256,1536]{2,1,0:T(8,128)(2,1)S(1)} async-done(((bf16[4,256,1536]{2,1,0:T(8,128)(2,1)}), bf16[4,256,1536]{2,1,0:T(8,128)(2,1)S(1)}, u32[]{:S(2)}, u32[]{:S(2)}) %all-to-all-start.2) | async-done | bytes 3145760 | tf_op jit(solution)/shard_map/all_to_all | solution.py:475
  362.2 2.3 collective-permute-done.49
  370.5 3.8 collective-permute-done.46
  375.3 3.9 collective-permute-done.50
  390.7 19.0 %attention_backward.1 = (f32[256,1024]{1,0:T(8,128)}, bf16[1024,2176]{1,0:T(8,128)(2,1)}, bf16[1024,1024]{1,0:T(8,128)(2,1)}) custom-call(s32[4]{0:T(128)} %bitcast.202, bf16[256,1024]{1,0:T(8,128)(2,1)} %token_ref.3, bf16[256,1024]{1,0:T(8,128)(2,1)} %dy_ref.1, bf16[1024,3200]{1,0:T(8,128)(2,1)} %bitcast.2.dense_ref, ...), custom_call_target="tpu_custom_call" | custom-call | flops 49999998976 | bytes 10000000 | tf_op jit(solution)/shard_map/attention_backward/pallas_call | solution.py:231
  415.8 4.9 all-to-all-start.3
  422.7 2.8 fusion
  431.4 12.6 %collective-permute-done.59 = bf16[4,2,32,1024]{3,2,1,0:T(8,128)(2,1)} collective-permute-done((bf16[4,2,32,1024]{3,2,1,0:T(8,128)(2,1)}, bf16[4,2,32,1024]{3,2,1,0:T(8,128)(2,1)}, u32[]{:S(2)}, u32[]{:S(2)}) %collective-permute-start.59) | collective-permute-done | bytes 524320 | tf_op jit(solution)/shard_map/ppermute | solution.py:248
  445.4 8.0 %collective-permute-done.56 = bf16[4,2,32,2176]{3,2,0,1:T(8,128)(2,1)} collective-permute-done((bf16[4,2,32,2176]{3,2,0,1:T(8,128)(2,1)}, bf16[4,2,32,2176]{3,2,0,1:T(8,128)(2,1)}, u32[]{:S(2)}, u32[]{:S(2)}) %collective-permute-start.56) | collective-permute-done | bytes 1114144 | tf_op jit(solution)/shard_map/ppermute | solution.py:248
  460.2 5.7 %collective-permute-done.60 = bf16[4,32,1024]{2,1,0:T(8,128)(2,1)} collective-permute-done((bf16[4,32,1024]{2,1,0:T(8,128)(2,1)S(1)}, bf16[4,32,1024]{2,1,0:T(8,128)(2,1)}, u32[]{:S(2)}, u32[]{:S(2)}) %collective-permute-start.60) | collective-permute-done | bytes 262176 | tf_op jit(solution)/shard_map/ppermute | solution.py:248
  467.0 4.1 collective-permute-done.57
  473.3 19.2 %all-to-all-done.3 = bf16[4,256,1536]{2,1,0:T(8,128)(2,1)} async-done(((bf16[4,256,1536]{2,1,0:T(8,128)(2,1)}), bf16[4,256,1536]{2,1,0:T(8,128)(2,1)}, u32[]{:S(2)}, u32[]{:S(2)}) %all-to-all-start.3) | async-done | bytes 3145760 | tf_op jit(solution)/shard_map/all_to_all | solution.py:475
  495.1 2.9 collective-permute-start.72
  498.0 2.3 convert_add_fusion.5
  507.2 2.7 fusion.27
  511.4 3.0 collective-permute-done.76
  515.4 3.4 collective-permute-done.77
  520.2 2.9 collective-permute-done.78
  523.8 3.6 collective-permute-done.79
  529.6 3.0 collective-permute-done.80
  533.1 4.6 collective-permute-done.81
  543.5 3.0 collective-permute-done.66
  550.9 5.2 collective-permute-done.69
  (386 shorter events, 232.7 us)
Async XLA Ops:
  7.4 15.3 %collective-permute-start = (bf16[1,1,32,3200]{3,2,1,0:T(8,128)(2,1)}, bf16[1,1,32,3200]{3,2,1,0:T(8,128)(2,1)}, u32[]{:S(2)}, u32[]{:S(2)}) collective-permute-start(bf16[1,1,32,3200]{3,2,1,0:T(8,128)(2,1)} %get-tuple-element.209), channel_id=1, source_target_pairs={{0,8},{8,0},{16,24},{24,16},{1,9},{9,1},{17,25},{25,17},{2,10},{10... | collective-permute-start | bytes 614408 | tf_op jit(solution)/shard_map/ppermute | solution.py:248
  10.4 18.0 %collective-permute-start.1 = (bf16[1,1,32,3200]{3,2,1,0:T(8,128)(2,1)}, bf16[1,1,32,3200]{3,2,1,0:T(8,128)(2,1)}, u32[]{:S(2)}, u32[]{:S(2)}) collective-permute-start(bf16[1,1,32,3200]{3,2,1,0:T(8,128)(2,1)} %get-tuple-element.209), channel_id=1, source_target_pairs={{0,16},{8,24},{16,0},{24,8},{1,17},{9,25},{17,1},{25,9},{2,18},{10... | collective-permute-start | bytes 614408 | tf_op jit(solution)/shard_map/ppermute | solution.py:248
  13.0 17.0 %collective-permute-start.2 = (bf16[1,1,32,3200]{3,2,1,0:T(8,128)(2,1)}, bf16[1,1,32,3200]{3,2,1,0:T(8,128)(2,1)}, u32[]{:S(2)}, u32[]{:S(2)}) collective-permute-start(bf16[1,1,32,3200]{3,2,1,0:T(8,128)(2,1)} %get-tuple-element.209), channel_id=1, source_target_pairs={{0,24},{8,16},{16,8},{24,0},{1,25},{9,17},{17,9},{25,1},{2,26},{10... | collective-permute-start | bytes 614408 | tf_op jit(solution)/shard_map/ppermute | solution.py:248
  13.9 32.0 %collective-permute-start.28 = (bf16[144,1024]{1,0:T(8,128)(2,1)}, bf16[144,1024]{1,0:T(8,128)(2,1)}, u32[]{:S(2)}, u32[]{:S(2)}) collective-permute-start(bf16[144,1024]{1,0:T(8,128)(2,1)} %get-tuple-element.231), channel_id=1, source_target_pairs={{0,2},{1,3},{2,0},{3,1},{4,6},{5,7},{6,4},{7,5},{8,10},{9,11},{10,... | collective-permute-start | bytes 884744 | tf_op jit(solution)/shard_map/ppermute | solution.py:248
  17.5 24.6 %collective-permute-start.29 = (bf16[128,1024]{1,0:T(8,128)(2,1)}, bf16[128,1024]{1,0:T(8,128)(2,1)}, u32[]{:S(2)}, u32[]{:S(2)}) collective-permute-start(bf16[128,1024]{1,0:T(8,128)(2,1)} %get-tuple-element.229), channel_id=1, source_target_pairs={{0,4},{1,5},{2,6},{3,7},{4,0},{5,1},{6,2},{7,3},{8,12},{9,13},{10,... | collective-permute-start | bytes 786440 | tf_op jit(solution)/shard_map/ppermute | solution.py:248
  31.6 42.1 %collective-permute-start.3 = (bf16[4,1,32,3200]{3,2,1,0:T(8,128)(2,1)}, bf16[4,1,32,3200]{3,2,1,0:T(8,128)(2,1)}, u32[]{:S(2)}, u32[]{:S(2)}) collective-permute-start(bf16[4,1,32,3200]{3,2,1,0:T(8,128)(2,1)} %constant_dynamic-update-slice_fusion.36), channel_id=1, source_target_pairs={{0,1},{1,0},{2,3},{3,2},{4,5},{5,4},{6,7},{7,6},{8,9},{9,8},{10,11... | collective-permute-start | bytes 2457608 | tf_op jit(solution)/shard_map/ppermute | solution.py:248
  33.7 16.3 %collective-permute-start.4 = (bf16[4,1,32,1536]{3,2,1,0:T(8,128)(2,1)S(1)}, bf16[4,1,32,1536]{3,2,1,0:T(8,128)(2,1)S(1)}, u32[]{:S(2)}, u32[]{:S(2)}) collective-permute-start(bf16[4,1,32,1536]{3,2,1,0:T(8,128)(2,1)S(1)} %slice.409), channel_id=1, source_target_pairs={{0,2},{1,3},{2,0},{3,1},{4,6},{5,7},{6,4},{7,5},{8,10},{9,11},{10,... | collective-permute-start | bytes 1179656 | tf_op jit(solution)/shard_map/ppermute | solution.py:248
  35.3 16.3 %collective-permute-start.6 = (bf16[4,1,32,1664]{3,2,1,0:T(8,128)(2,1)S(1)}, bf16[4,1,32,1664]{3,2,1,0:T(8,128)(2,1)S(1)}, u32[]{:S(2)}, u32[]{:S(2)}) collective-permute-start(bf16[4,1,32,1664]{3,2,1,0:T(8,128)(2,1)S(1)} %slice.410), channel_id=1, source_target_pairs={{0,4},{1,5},{2,6},{3,7},{4,0},{5,1},{6,2},{7,3},{8,12},{9,13},{10,... | collective-permute-start | bytes 1277960 | tf_op jit(solution)/shard_map/ppermute | solution.py:248
  42.1 14.7 %collective-permute-start.12 = (bf16[272,1024]{1,0:T(8,128)(2,1)S(1)}, bf16[272,1024]{1,0:T(8,128)(2,1)S(1)}, u32[]{:S(2)}, u32[]{:S(2)}) collective-permute-start(bf16[272,1024]{1,0:T(8,128)(2,1)S(1)} %copy-done.21), channel_id=1, source_target_pairs={{0,8},{8,0},{16,24},{24,16},{1,9},{9,1},{17,25},{25,17},{2,10},{10... | collective-permute-start | bytes 1671176 | tf_op jit(solution)/shard_map/ppermute | solution.py:248
  45.9 18.6 %collective-permute-start.30 = (bf16[256,1024]{1,0:T(8,128)(2,1)}, bf16[256,1024]{1,0:T(8,128)(2,1)}, u32[]{:S(2)}, u32[]{:S(2)}) collective-permute-start(bf16[256,1024]{1,0:T(8,128)(2,1)} %pad_maximum_fusion.22), channel_id=1, source_target_pairs={{0,2},{1,3},{2,0},{3,1},{4,6},{5,7},{6,4},{7,5},{8,10},{9,11},{10,... | collective-permute-start | bytes 1572872 | tf_op jit(solution)/shard_map/ppermute | solution.py:248
  50.1 16.7 %collective-permute-start.31 = (bf16[288,1024]{1,0:T(8,128)(2,1)}, bf16[288,1024]{1,0:T(8,128)(2,1)}, u32[]{:S(2)}, u32[]{:S(2)}) collective-permute-start(bf16[288,1024]{1,0:T(8,128)(2,1)} %pad_maximum_fusion.15), channel_id=1, source_target_pairs={{0,4},{1,5},{2,6},{3,7},{4,0},{5,1},{6,2},{7,3},{8,12},{9,13},{10,... | collective-permute-start | bytes 1769480 | tf_op jit(solution)/shard_map/ppermute | solution.py:248
  51.6 30.2 %collective-permute-start.8 = (bf16[4,2,32,1536]{3,2,1,0:T(8,128)(2,1)}, bf16[4,2,32,1536]{3,2,1,0:T(8,128)(2,1)}, u32[]{:S(2)}, u32[]{:S(2)}) collective-permute-start(bf16[4,2,32,1536]{3,2,1,0:T(8,128)(2,1)} %pad_maximum_fusion.11), channel_id=1, source_target_pairs={{0,4},{1,5},{2,6},{3,7},{4,0},{5,1},{6,2},{7,3},{8,12},{9,13},{10,... | collective-permute-start | bytes 2359304 | tf_op jit(solution)/shard_map/ppermute | solution.py:248
  57.6 19.4 %collective-permute-start.5 = (bf16[4,1,32,1536]{3,2,1,0:T(8,128)(2,1)S(1)}, bf16[4,1,32,1536]{3,2,1,0:T(8,128)(2,1)}, u32[]{:S(2)}, u32[]{:S(2)}) collective-permute-start(bf16[4,1,32,1536]{3,2,1,0:T(8,128)(2,1)S(1)} %collective-permute-done.4), channel_id=1, source_target_pairs={{0,1},{1,0},{2,3},{3,2},{4,5},{5,4},{6,7},{7,6},{8,9},{9,8},{10,11... | collective-permute-start | bytes 1179656 | tf_op jit(solution)/shard_map/ppermute | solution.py:248
  59.6 98.5 %all-to-all-start = ((bf16[4,256,1536]{2,1,0:T(8,128)(2,1)}), bf16[4,256,1536]{2,1,0:T(8,128)(2,1)}, u32[]{:S(2)}, u32[]{:S(2)}) async-start(bf16[4,256,1536]{2,1,0:T(8,128)(2,1)} %pad_maximum_fusion.2), calls=%async_computation | async-start | bytes 6291456 | tf_op jit(solution)/shard_map/all_to_all | solution.py:470
  64.5 21.6 %collective-permute-start.10 = (bf16[4,2,32,1664]{3,2,1,0:T(8,128)(2,1)}, bf16[4,2,32,1664]{3,2,1,0:T(8,128)(2,1)S(1)}, u32[]{:S(2)}, u32[]{:S(2)}) collective-permute-start(bf16[4,2,32,1664]{3,2,1,0:T(8,128)(2,1)} %pad_maximum_fusion.10), channel_id=1, source_target_pairs={{0,2},{1,3},{2,0},{3,1},{4,6},{5,7},{6,4},{7,5},{8,10},{9,11},{10,... | collective-permute-start | bytes 2555912 | tf_op jit(solution)/shard_map/ppermute | solution.py:248
  66.7 15.9 %collective-permute-start.7 = (bf16[4,1,32,1664]{3,2,1,0:T(8,128)(2,1)}, bf16[4,1,32,1664]{3,2,1,0:T(8,128)(2,1)S(1)}, u32[]{:S(2)}, u32[]{:S(2)}) collective-permute-start(bf16[4,1,32,1664]{3,2,1,0:T(8,128)(2,1)} %copy-done.17), channel_id=1, source_target_pairs={{0,1},{1,0},{2,3},{3,2},{4,5},{5,4},{6,7},{7,6},{8,9},{9,8},{10,11... | collective-permute-start | bytes 1277960 | tf_op jit(solution)/shard_map/ppermute | solution.py:248
  73.7 122.0 %collective-permute-start.32 = (bf16[1088,1024]{1,0:T(8,128)(2,1)}, bf16[1088,1024]{1,0:T(8,128)(2,1)}, u32[]{:S(2)}, u32[]{:S(2)}) collective-permute-start(bf16[1088,1024]{1,0:T(8,128)(2,1)} %slice_dynamic-update-slice_fusion.16.refs_4_), channel_id=1, source_target_pairs={{0,1},{1,0},{2,3},{3,2},{4,5},{5,4},{6,7},{7,6},{8,9},{9,8},{10,11... | collective-permute-start | bytes 6684680 | tf_op jit(solution)/shard_map/ppermute | solution.py:248
  93.6 14.8 %collective-permute-start.14 = (bf16[128,1024]{1,0:T(8,128)(2,1)}, bf16[128,1024]{1,0:T(8,128)(2,1)}, u32[]{:S(2)}, u32[]{:S(2)}) collective-permute-start(bf16[128,1024]{1,0:T(8,128)(2,1)} %slice.327), channel_id=1, source_target_pairs={{0,4},{1,5},{2,6},{3,7},{4,0},{5,1},{6,2},{7,3},{8,12},{9,13},{10,... | collective-permute-start | bytes 786440 | tf_op jit(solution)/shard_map/ppermute | solution.py:248
  110.3 17.4 %collective-permute-start.15 = (bf16[256,1024]{1,0:T(8,128)(2,1)}, bf16[256,1024]{1,0:T(8,128)(2,1)}, u32[]{:S(2)}, u32[]{:S(2)}) collective-permute-start(bf16[256,1024]{1,0:T(8,128)(2,1)} %pad_maximum_fusion.19), channel_id=1, source_target_pairs={{0,2},{1,3},{2,0},{3,1},{4,6},{5,7},{6,4},{7,5},{8,10},{9,11},{10,... | collective-permute-start | bytes 1572872 | tf_op jit(solution)/shard_map/ppermute | solution.py:248
  119.0 14.3 %collective-permute-start.16 = (bf16[288,1024]{1,0:T(8,128)(2,1)}, bf16[288,1024]{1,0:T(8,128)(2,1)}, u32[]{:S(2)}, u32[]{:S(2)}) collective-permute-start(bf16[288,1024]{1,0:T(8,128)(2,1)} %pad_maximum_fusion.12), channel_id=1, source_target_pairs={{0,4},{1,5},{2,6},{3,7},{4,0},{5,1},{6,2},{7,3},{8,12},{9,13},{10,... | collective-permute-start | bytes 1769480 | tf_op jit(solution)/shard_map/ppermute | solution.py:248
  133.3 21.7 %collective-permute-start.22 = (bf16[272,1024]{1,0:T(8,128)(2,1)S(1)}, bf16[272,1024]{1,0:T(8,128)(2,1)S(1)}, u32[]{:S(2)}, u32[]{:S(2)}) collective-permute-start(bf16[272,1024]{1,0:T(8,128)(2,1)S(1)} %maximum_maximum_fusion), channel_id=1, source_target_pairs={{0,8},{8,0},{16,24},{24,16},{1,9},{9,1},{17,25},{25,17},{2,10},{10... | collective-permute-start | bytes 1671176 | tf_op jit(solution)/shard_map/ppermute | solution.py:248
  135.1 17.8 %collective-permute-start.17 = (bf16[144,1024]{1,0:T(8,128)(2,1)S(1)}, bf16[144,1024]{1,0:T(8,128)(2,1)S(1)}, u32[]{:S(2)}, u32[]{:S(2)}) collective-permute-start(bf16[144,1024]{1,0:T(8,128)(2,1)S(1)} %slice.328), channel_id=1, source_target_pairs={{0,2},{1,3},{2,0},{3,1},{4,6},{5,7},{6,4},{7,5},{8,10},{9,11},{10,... | collective-permute-start | bytes 884744 | tf_op jit(solution)/shard_map/ppermute | solution.py:248
  135.5 14.9 %collective-permute-start.18 = (bf16[128,1024]{1,0:T(8,128)(2,1)S(1)}, bf16[128,1024]{1,0:T(8,128)(2,1)S(1)}, u32[]{:S(2)}, u32[]{:S(2)}) collective-permute-start(bf16[128,1024]{1,0:T(8,128)(2,1)S(1)} %slice.329), channel_id=1, source_target_pairs={{0,4},{1,5},{2,6},{3,7},{4,0},{5,1},{6,2},{7,3},{8,12},{9,13},{10,... | collective-permute-start | bytes 786440 | tf_op jit(solution)/shard_map/ppermute | solution.py:248
  149.7 46.1 %collective-permute-start.33 = (bf16[1088,1024]{1,0:T(8,128)(2,1)}, bf16[1088,1024]{1,0:T(8,128)(2,1)}, u32[]{:S(2)}, u32[]{:S(2)}) collective-permute-start(bf16[1088,1024]{1,0:T(8,128)(2,1)} %slice_dynamic-update-slice_fusion.22.refs_6_), channel_id=1, source_target_pairs={{0,1},{1,0},{2,3},{3,2},{4,5},{5,4},{6,7},{7,6},{8,9},{9,8},{10,11... | collective-permute-start | bytes 6684680 | tf_op jit(solution)/shard_map/ppermute | solution.py:248
  151.4 14.7 %collective-permute-start.19 = (bf16[256,1024]{1,0:T(8,128)(2,1)}, bf16[256,1024]{1,0:T(8,128)(2,1)}, u32[]{:S(2)}, u32[]{:S(2)}) collective-permute-start(bf16[256,1024]{1,0:T(8,128)(2,1)} %pad_maximum_fusion.20), channel_id=1, source_target_pairs={{0,2},{1,3},{2,0},{3,1},{4,6},{5,7},{6,4},{7,5},{8,10},{9,11},{10,... | collective-permute-start | bytes 1572872 | tf_op jit(solution)/shard_map/ppermute | solution.py:248
  153.7 24.4 %collective-permute-start.20 = (bf16[288,1024]{1,0:T(8,128)(2,1)}, bf16[288,1024]{1,0:T(8,128)(2,1)}, u32[]{:S(2)}, u32[]{:S(2)}) collective-permute-start(bf16[288,1024]{1,0:T(8,128)(2,1)} %pad_maximum_fusion.13), channel_id=1, source_target_pairs={{0,4},{1,5},{2,6},{3,7},{4,0},{5,1},{6,2},{7,3},{8,12},{9,13},{10,... | collective-permute-start | bytes 1769480 | tf_op jit(solution)/shard_map/ppermute | solution.py:248
  155.7 19.4 %collective-permute-start.24 = (bf16[128,1024]{1,0:T(8,128)(2,1)}, bf16[128,1024]{1,0:T(8,128)(2,1)}, u32[]{:S(2)}, u32[]{:S(2)}) collective-permute-start(bf16[128,1024]{1,0:T(8,128)(2,1)} %slice.424), channel_id=1, source_target_pairs={{0,4},{1,5},{2,6},{3,7},{4,0},{5,1},{6,2},{7,3},{8,12},{9,13},{10,... | collective-permute-start | bytes 786440 | tf_op jit(solution)/shard_map/ppermute | solution.py:248
  160.1 78.2 %all-to-all-start.1 = ((bf16[4,256,1536]{2,1,0:T(8,128)(2,1)}), bf16[4,256,1536]{2,1,0:T(8,128)(2,1)S(1)}, u32[]{:S(2)}, u32[]{:S(2)}) async-start(bf16[4,256,1536]{2,1,0:T(8,128)(2,1)} %pad_maximum_fusion.3), calls=%async_computation.1 | async-start | bytes 6291456 | tf_op jit(solution)/shard_map/all_to_all | solution.py:470
  176.8 14.4 %collective-permute-start.26 = (bf16[288,1024]{1,0:T(8,128)(2,1)S(1)}, bf16[288,1024]{1,0:T(8,128)(2,1)S(1)}, u32[]{:S(2)}, u32[]{:S(2)}) collective-permute-start(bf16[288,1024]{1,0:T(8,128)(2,1)S(1)} %pad_maximum_fusion.14), channel_id=1, source_target_pairs={{0,4},{1,5},{2,6},{3,7},{4,0},{5,1},{6,2},{7,3},{8,12},{9,13},{10,... | collective-permute-start | bytes 1769480 | tf_op jit(solution)/shard_map/ppermute | solution.py:248
  279.9 74.9 %all-to-all-start.2 = ((bf16[4,256,1536]{2,1,0:T(8,128)(2,1)}), bf16[4,256,1536]{2,1,0:T(8,128)(2,1)S(1)}, u32[]{:S(2)}, u32[]{:S(2)}) async-start(bf16[4,256,1536]{2,1,0:T(8,128)(2,1)} %bitcast.196), calls=%async_computation.2 | async-start | bytes 6291456 | tf_op jit(solution)/shard_map/all_to_all | solution.py:475
  290.7 48.9 %collective-permute-start.35 = (bf16[2,144,1024]{2,1,0:T(8,128)(2,1)S(1)}, bf16[2,144,1024]{2,1,0:T(8,128)(2,1)S(1)}, u32[]{:S(2)}, u32[]{:S(2)}) collective-permute-start(bf16[2,144,1024]{2,1,0:T(8,128)(2,1)S(1)} %slice_bitcast_fusion.6), channel_id=1, source_target_pairs={{0,4},{1,5},{2,6},{3,7},{4,0},{5,1},{6,2},{7,3},{8,12},{9,13},{10,... | collective-permute-start | bytes 1769480 | tf_op jit(solution)/shard_map/ppermute | solution.py:248
  291.2 14.8 %collective-permute-start.36 = (bf16[2,128,1024]{2,1,0:T(8,128)(2,1)S(1)}, bf16[2,128,1024]{2,1,0:T(8,128)(2,1)S(1)}, u32[]{:S(2)}, u32[]{:S(2)}) collective-permute-start(bf16[2,128,1024]{2,1,0:T(8,128)(2,1)S(1)} %slice_bitcast_fusion.14), channel_id=1, source_target_pairs={{0,2},{1,3},{2,0},{3,1},{4,6},{5,7},{6,4},{7,5},{8,10},{9,11},{10,... | collective-permute-start | bytes 1572872 | tf_op jit(solution)/shard_map/ppermute | solution.py:248
  292.7 47.9 %collective-permute-start.38 = (bf16[2,144,1024]{2,1,0:T(8,128)(2,1)S(1)}, bf16[2,144,1024]{2,1,0:T(8,128)(2,1)S(1)}, u32[]{:S(2)}, u32[]{:S(2)}) collective-permute-start(bf16[2,144,1024]{2,1,0:T(8,128)(2,1)S(1)} %slice_bitcast_fusion.4), channel_id=1, source_target_pairs={{0,4},{1,5},{2,6},{3,7},{4,0},{5,1},{6,2},{7,3},{8,12},{9,13},{10,... | collective-permute-start | bytes 1769480 | tf_op jit(solution)/shard_map/ppermute | solution.py:248
  294.3 23.0 %collective-permute-start.39 = (bf16[2,128,1024]{2,1,0:T(8,128)(2,1)S(1)}, bf16[2,128,1024]{2,1,0:T(8,128)(2,1)S(1)}, u32[]{:S(2)}, u32[]{:S(2)}) collective-permute-start(bf16[2,128,1024]{2,1,0:T(8,128)(2,1)S(1)} %slice_bitcast_fusion.12), channel_id=1, source_target_pairs={{0,2},{1,3},{2,0},{3,1},{4,6},{5,7},{6,4},{7,5},{8,10},{9,11},{10,... | collective-permute-start | bytes 1572872 | tf_op jit(solution)/shard_map/ppermute | solution.py:248
  296.0 45.7 %collective-permute-start.41 = (bf16[2,144,1024]{2,1,0:T(8,128)(2,1)S(1)}, bf16[2,144,1024]{2,1,0:T(8,128)(2,1)S(1)}, u32[]{:S(2)}, u32[]{:S(2)}) collective-permute-start(bf16[2,144,1024]{2,1,0:T(8,128)(2,1)S(1)} %slice_bitcast_fusion.2), channel_id=1, source_target_pairs={{0,4},{1,5},{2,6},{3,7},{4,0},{5,1},{6,2},{7,3},{8,12},{9,13},{10,... | collective-permute-start | bytes 1769480 | tf_op jit(solution)/shard_map/ppermute | solution.py:248
  306.0 22.5 %collective-permute-start.42 = (bf16[2,128,1024]{2,1,0:T(8,128)(2,1)S(1)}, bf16[2,128,1024]{2,1,0:T(8,128)(2,1)S(1)}, u32[]{:S(2)}, u32[]{:S(2)}) collective-permute-start(bf16[2,128,1024]{2,1,0:T(8,128)(2,1)S(1)} %slice_bitcast_fusion.10), channel_id=1, source_target_pairs={{0,2},{1,3},{2,0},{3,1},{4,6},{5,7},{6,4},{7,5},{8,10},{9,11},{10,... | collective-permute-start | bytes 1572872 | tf_op jit(solution)/shard_map/ppermute | solution.py:248
  317.3 21.3 %collective-permute-start.45 = (bf16[2,128,1024]{2,1,0:T(8,128)(2,1)S(1)}, bf16[2,128,1024]{2,1,0:T(8,128)(2,1)S(1)}, u32[]{:S(2)}, u32[]{:S(2)}) collective-permute-start(bf16[2,128,1024]{2,1,0:T(8,128)(2,1)S(1)} %slice_bitcast_fusion.8), channel_id=1, source_target_pairs={{0,2},{1,3},{2,0},{3,1},{4,6},{5,7},{6,4},{7,5},{8,10},{9,11},{10,... | collective-permute-start | bytes 1572872 | tf_op jit(solution)/shard_map/ppermute | solution.py:248
  328.5 15.5 %collective-permute-start.44 = (bf16[2,144,1024]{2,1,0:T(8,128)(2,1)S(1)}, bf16[2,144,1024]{2,1,0:T(8,128)(2,1)S(1)}, u32[]{:S(2)}, u32[]{:S(2)}) collective-permute-start(bf16[2,144,1024]{2,1,0:T(8,128)(2,1)S(1)} %slice_bitcast_fusion), channel_id=1, source_target_pairs={{0,4},{1,5},{2,6},{3,7},{4,0},{5,1},{6,2},{7,3},{8,12},{9,13},{10,... | collective-permute-start | bytes 1769480 | tf_op jit(solution)/shard_map/ppermute | solution.py:248
  383.4 26.3 %collective-permute-start.52 = (bf16[128,1024]{1,0:T(8,128)(2,1)S(1)}, bf16[128,1024]{1,0:T(8,128)(2,1)S(1)}, u32[]{:S(2)}, u32[]{:S(2)}) collective-permute-start(bf16[128,1024]{1,0:T(8,128)(2,1)S(1)} %slice_bitcast_fusion.21), channel_id=1, source_target_pairs={{0,4},{1,5},{2,6},{3,7},{4,0},{5,1},{6,2},{7,3},{8,12},{9,13},{10,... | collective-permute-start | bytes 786440 | tf_op jit(solution)/shard_map/ppermute | solution.py:248
  385.9 23.9 %collective-permute-start.51 = (bf16[144,1024]{1,0:T(8,128)(2,1)S(1)}, bf16[144,1024]{1,0:T(8,128)(2,1)S(1)}, u32[]{:S(2)}, u32[]{:S(2)}) collective-permute-start(bf16[144,1024]{1,0:T(8,128)(2,1)S(1)} %slice_bitcast_fusion.17), channel_id=1, source_target_pairs={{0,2},{1,3},{2,0},{3,1},{4,6},{5,7},{6,4},{7,5},{8,10},{9,11},{10,... | collective-permute-start | bytes 884744 | tf_op jit(solution)/shard_map/ppermute | solution.py:248
  388.5 21.2 %collective-permute-start.54 = (bf16[128,1024]{1,0:T(8,128)(2,1)S(1)}, bf16[128,1024]{1,0:T(8,128)(2,1)S(1)}, u32[]{:S(2)}, u32[]{:S(2)}) collective-permute-start(bf16[128,1024]{1,0:T(8,128)(2,1)S(1)} %slice_bitcast_fusion.20), channel_id=1, source_target_pairs={{0,4},{1,5},{2,6},{3,7},{4,0},{5,1},{6,2},{7,3},{8,12},{9,13},{10,... | collective-permute-start | bytes 786440 | tf_op jit(solution)/shard_map/ppermute | solution.py:248
  390.1 20.7 %collective-permute-start.53 = (bf16[144,1024]{1,0:T(8,128)(2,1)S(1)}, bf16[144,1024]{1,0:T(8,128)(2,1)S(1)}, u32[]{:S(2)}, u32[]{:S(2)}) collective-permute-start(bf16[144,1024]{1,0:T(8,128)(2,1)S(1)} %slice_bitcast_fusion.16), channel_id=1, source_target_pairs={{0,2},{1,3},{2,0},{3,1},{4,6},{5,7},{6,4},{7,5},{8,10},{9,11},{10,... | collective-permute-start | bytes 884744 | tf_op jit(solution)/shard_map/ppermute | solution.py:248
  415.8 76.6 %all-to-all-start.3 = ((bf16[4,256,1536]{2,1,0:T(8,128)(2,1)}), bf16[4,256,1536]{2,1,0:T(8,128)(2,1)}, u32[]{:S(2)}, u32[]{:S(2)}) async-start(bf16[4,256,1536]{2,1,0:T(8,128)(2,1)} %bitcast.195), calls=%async_computation.3 | async-start | bytes 6291456 | tf_op jit(solution)/shard_map/all_to_all | solution.py:475
  426.6 26.8 %collective-permute-start.56 = (bf16[4,2,32,2176]{3,2,0,1:T(8,128)(2,1)}, bf16[4,2,32,2176]{3,2,0,1:T(8,128)(2,1)}, u32[]{:S(2)}, u32[]{:S(2)}) collective-permute-start(bf16[4,2,32,2176]{3,2,0,1:T(8,128)(2,1)} %dynamic-slice_bitcast_fusion), channel_id=1, source_target_pairs={{0,4},{1,5},{2,6},{3,7},{4,0},{5,1},{6,2},{7,3},{8,12},{9,13},{10,... | collective-permute-start | bytes 3342344 | tf_op jit(solution)/shard_map/ppermute | solution.py:248
  502.7 57.5 %collective-permute-start.61 = (bf16[272,1024]{1,0:T(8,128)(2,1)}, bf16[272,1024]{1,0:T(8,128)(2,1)}, u32[]{:S(2)}, u32[]{:S(2)}) collective-permute-start(bf16[272,1024]{1,0:T(8,128)(2,1)} %pad_maximum_fusion.17), channel_id=1, source_target_pairs={{0,8},{8,0},{16,24},{24,16},{1,9},{9,1},{17,25},{25,17},{2,10},{10... | collective-permute-start | bytes 1671176 | tf_op jit(solution)/shard_map/ppermute | solution.py:248
  502.7 35.0 %collective-permute-start.64 = (bf16[1,32,2176]{2,1,0:T(8,128)(2,1)S(1)}, bf16[1,32,2176]{2,1,0:T(8,128)(2,1)S(1)}, u32[]{:S(2)}, u32[]{:S(2)}) collective-permute-start(bf16[1,32,2176]{2,1,0:T(8,128)(2,1)S(1)} %get-tuple-element.227), channel_id=1, source_target_pairs={{0,24},{8,16},{16,8},{24,0},{1,25},{9,17},{17,9},{25,1},{2,26},{10... | collective-permute-start | bytes 417800 | tf_op jit(solution)/shard_map/ppermute | solution.py:248
  504.1 33.6 %collective-permute-start.63 = (bf16[1,32,2176]{2,1,0:T(8,128)(2,1)S(1)}, bf16[1,32,2176]{2,1,0:T(8,128)(2,1)S(1)}, u32[]{:S(2)}, u32[]{:S(2)}) collective-permute-start(bf16[1,32,2176]{2,1,0:T(8,128)(2,1)S(1)} %get-tuple-element.228), channel_id=1, source_target_pairs={{0,16},{8,24},{16,0},{24,8},{1,17},{9,25},{17,1},{25,9},{2,18},{10... | collective-permute-start | bytes 417800 | tf_op jit(solution)/shard_map/ppermute | solution.py:248
  506.2 31.6 %collective-permute-start.62 = (bf16[1,32,2176]{2,1,0:T(8,128)(2,1)S(1)}, bf16[1,32,2176]{2,1,0:T(8,128)(2,1)S(1)}, u32[]{:S(2)}, u32[]{:S(2)}) collective-permute-start(bf16[1,32,2176]{2,1,0:T(8,128)(2,1)S(1)} %get-tuple-element.226), channel_id=1, source_target_pairs={{0,8},{8,0},{16,24},{24,16},{1,9},{9,1},{17,25},{25,17},{2,10},{10... | collective-permute-start | bytes 417800 | tf_op jit(solution)/shard_map/ppermute | solution.py:248
  (68 other events, 534.4 us)
